TPU v7x, 256 devices: a whole 4x4x8 slice. The times are simulated.
256 devices in a mesh: feat: 4 (over y_lo, core), row: 4 (over x), col: 16 (over z, y_hi).
Axes of the slice: x: 4, y: 4 (y_hi: 2, y_lo: 2; y = y_hi * 2 + y_lo), z: 8, core: 2. Of those that a mesh axis runs over, the one named last changes fastest.
Arguments:
- features: bfloat16 [24576, 768], P('col', 'feat'), may hold values from -6 to 6
- weight: bfloat16 [768, 256], P('feat'), may hold values from -0.21875 to 0.21875
- tile_values: bfloat16 [4, 16, 64, 128, 128], P('row', 'col'), as said below
- tile_rows: int32 [4, 16, 64], P('row', 'col'), may hold values from 0 to 47, as said below
- tile_cols: int32 [4, 16, 64], P('row', 'col'), may hold values from 0 to 11
- tile_count: int32 [4, 16], P('row', 'col'), may hold values from 1 to 64, as said below
- cotangent: bfloat16 [24576, 256], P(('row', 'col')), may hold values from -6 to 6
Outputs:
- activated: bfloat16 [24576, 256], P(('row', 'col'))
- feature_grad: bfloat16 [16, 1536, 768], P('col', 'row', 'feat')
- weight_grad: float32 [768, 256], P('feat')
Inputs may be any that keep to these rules, and one draw needn't show every extreme that they name: Within one block (r, c) the pairs (tile_rows, tile_cols) of all slots are distinct. `tile_count`: some block has all 64 slots live. `tile_values`: entries are nonnegative.
All inputs are finite; a program needn't handle non-finite values.
Results may differ from a plain program's by a relative error of at most 0.025.
Values may be sent and summed in bfloat16 or wider, within the bound.
A program may use at most 128 MiB of HBM per device.

v0:
```python
import math

import jax
import jax.numpy as jnp
from jax import lax
from jax.sharding import PartitionSpec as P


def silu_slope(values):
    sigma = jax.nn.sigmoid(values)
    return sigma * (1.0 + values * (1.0 - sigma))


def shards(features, weight, tile_values, tile_rows, tile_cols, tile_count, cotangent):
    tile_size = tile_values.shape[-1]
    slot_count = tile_values.shape[2]
    node_dev = cotangent.shape[0]
    width = features.shape[1]
    col_tiles = features.shape[0] // tile_size
    row_tiles = node_dev * lax.axis_size("col") // tile_size
    live = (jnp.arange(slot_count)[:, None, None] < tile_count[0, 0]).astype(jnp.bfloat16)
    values = tile_values[0, 0] * live
    rows_index = tile_rows[0, 0]
    cols_index = tile_cols[0, 0]
    place = rows_index * col_tiles + cols_index
    dense = (
        jnp.zeros((row_tiles * col_tiles, tile_size, tile_size), jnp.bfloat16).at[place].set(values)
    )
    dense = dense.reshape(row_tiles, col_tiles, tile_size, tile_size)
    blocks = features.reshape(col_tiles, tile_size, width)
    partial_sum = jnp.einsum("rcij,cjf->rif", dense, blocks, preferred_element_type=jnp.float32)
    partial_sum = partial_sum.reshape(row_tiles * tile_size, width)
    partial_sum = lax.optimization_barrier(partial_sum.astype(jnp.bfloat16)).astype(jnp.float32)
    aggregated = lax.psum_scatter(
        partial_sum.astype(jnp.bfloat16), "col", scatter_dimension=0, tiled=True
    )
    hidden_part = jnp.dot(aggregated, weight, preferred_element_type=jnp.float32)
    hidden = lax.psum(hidden_part.astype(jnp.bfloat16), "feat").astype(jnp.float32)
    activated = jax.nn.silu(hidden).astype(jnp.bfloat16)
    hidden_grad = (cotangent.astype(jnp.float32) * silu_slope(hidden)).astype(jnp.bfloat16)
    nodes_total = node_dev * lax.axis_size("row") * lax.axis_size("col")
    weight_part = jnp.dot(aggregated.T, hidden_grad, preferred_element_type=jnp.float32)
    weight_grad = lax.psum(weight_part, ("row", "col")) * (1.0 / math.sqrt(nodes_total))
    gathered = jnp.dot(
        lax.all_gather(hidden_grad, "col", axis=0, tiled=True),
        weight.T,
        preferred_element_type=jnp.float32,
    ).astype(jnp.bfloat16)
    targets = gathered.reshape(row_tiles, tile_size, width)
    back_sum = jnp.einsum("rcij,rif->cjf", dense, targets, preferred_element_type=jnp.float32)
    back_sum = back_sum.reshape(col_tiles * tile_size, width)
    back_sum = lax.optimization_barrier(back_sum.astype(jnp.bfloat16)).astype(jnp.float32)
    feature_grad = lax.psum_scatter(
        back_sum.astype(jnp.bfloat16), "row", scatter_dimension=0, tiled=True
    )
    feature_grad = feature_grad.reshape(1, node_dev, width)
    return (activated, feature_grad, weight_grad)


def solution(mesh):
    return jax.shard_map(
        shards,
        mesh=mesh,
        in_specs=(
            P("col", "feat"),
            P("feat", None),
            P("row", "col", None, None, None),
            P("row", "col", None),
            P("row", "col", None),
            P("row", "col"),
            P(("row", "col"), None),
        ),
        out_specs=(P(("row", "col"), None), P("col", "row", "feat"), P("feat", None)),
        check_vma=False,
    )
```

profile of v0, /device:TPU:1, one launch (start us, length us, event | category | flops | bytes accessed | tf_op | source)
XLA Modules:
  0.0 1057.7 jit_solution(8151269328651877644)
XLA Ops:
  7.2 0.0 copy-start
  7.2 0.0 reduce-scatter.7.cloned.1.call-start
  7.9 0.7 fusion.15
  8.6 1.8 bitcast_multiply_fusion
  10.4 7.1 broadcast_in_dim.2
  17.5 8.7 scatter_fusion
  26.3 9.6 copy.17
  35.9 0.0 copy-done
  35.9 6.4 fusion
  42.4 0.0 copy-start.4
  42.4 2.8 copy.21
  45.1 0.0 copy-start.5
  45.1 0.0 reduce-scatter.7.cloned.1.call-update
  45.2 0.0 all-reduce.3.cloned.1.call-start
  45.2 210.0 %reduce-scatter.7.cloned.1.call-done = bf16[384,192]{1,0:T(8,128)(2,1)} async-done(((bf16[6144,192]{1,0:T(8,128)(2,1)}), bf16[384,192]{1,0:T(8,128)(2,1)}) %reduce-scatter.7.cloned.1.call-update) | async-done | bytes 147472
  255.2 0.0 copy-done.4
  255.2 1.8 convolution_convert_fusion.1
  257.0 0.0 all-reduce.3.cloned.1.call-update
  257.0 0.0 all-gather.2.cloned.1.call-start
  257.1 45.0 %all-reduce.3.cloned.1.call-done = bf16[384,256]{1,0:T(8,128)(2,1)} async-done(((bf16[384,256]{1,0:T(8,128)(2,1)}), bf16[384,256]{1,0:T(8,128)(2,1)}) %all-reduce.3.cloned.1.call-update) | async-done | bytes 196624 | tf_op jit(solution)/shard_map/psum | solution.py:38
  302.1 0.0 copy-done.5
  302.1 1.8 fusion.14
  304.0 0.0 all-gather.2.cloned.1.call-update
  304.0 0.0 all-reduce.5.cloned.1.call-start
  304.0 0.0 copy-start.2
  304.0 0.0 copy-start.3
  304.1 24.7 %copy.19 = bf16[12,128,128,48]{2,1,0,3:T(8,128)(2,1)} copy(bf16[12,128,128,48]{1,2,0,3:T(8,128)(2,1)} %bitcast.47) | data formatting | bytes 37748736 | tf_op jit(solution)/shard_map/rcij,rif->cjf/dot_general | solution.py:50
  328.7 0.0 copy-done.2
  328.7 0.0 copy-done.3
  328.7 0.9 fusion.16
  329.7 0.0 all-reduce.5.cloned.1.call-update
  329.7 0.0 reduce-scatter.9.cloned.1.call-start
  329.7 65.7 %all-gather.2.cloned.1.call-done = bf16[6144,256]{1,0:T(8,128)(2,1)} async-done(((bf16[384,256]{1,0:T(8,128)(2,1)}), bf16[6144,256]{1,0:T(8,128)(2,1)}) %all-gather.2.cloned.1.call-update) | async-done | bytes 3145744 | tf_op jit(solution)/shard_map/all_gather | solution.py:45
  395.5 3.1 fusion.4
  398.5 0.0 copy-start.1
  398.6 10.3 fusion.1
  408.8 1.2 copy.23
  410.0 0.0 reduce-scatter.9.cloned.1.call-update
  410.0 590.6 %all-reduce.5.cloned.1.call-done = f32[192,256]{1,0:T(8,128)} async-done(((f32[192,256]{1,0:T(8,128)}), f32[192,256]{1,0:T(8,128)}) %all-reduce.5.cloned.1.call-update) | async-done | bytes 196624 | tf_op jit(solution)/shard_map/psum | solution.py:43
  1000.6 1.6 broadcast_multiply_fusion
  1002.2 47.3 %reduce-scatter.9.cloned.1.call-done = bf16[384,192]{1,0:T(8,128)(2,1)} async-done(((bf16[1536,192]{1,0:T(8,128)(2,1)}), bf16[384,192]{1,0:T(8,128)(2,1)}) %reduce-scatter.9.cloned.1.call-update) | async-done | bytes 147472
  1049.4 1.7 copy.24
  1051.2 0.0 copy-done.1
  (1 shorter events, 0.0 us)
Async XLA Ops:
  7.2 28.7 %copy-start = (bf16[1536,192]{0,1:T(8,128)(2,1)S(1)}, bf16[1536,192]{0,1:T(8,128)(2,1)}, u32[]{:S(2)}) copy-start(bf16[1536,192]{0,1:T(8,128)(2,1)} %param.7) | copy-start | bytes 1769476
  7.2 248.0 %reduce-scatter.7.cloned.1.call-start = ((), (), s32[]{:S(2)}) async-start(), calls=%async_computation.5 | async-start | bytes 3342336
  42.4 212.8 %copy-start.4 = (bf16[192,256]{1,0:T(8,128)(2,1)S(1)}, bf16[192,256]{1,0:T(8,128)(2,1)}, u32[]{:S(2)}) copy-start(bf16[192,256]{1,0:T(8,128)(2,1)} %param.8) | copy-start | bytes 294916
  45.1 257.0 %copy-start.5 = (bf16[384,256]{1,0:T(8,128)(2,1)S(1)}, bf16[384,256]{1,0:T(8,128)(2,1)}, u32[]{:S(2)}) copy-start(bf16[384,256]{1,0:T(8,128)(2,1)} %param.13) | copy-start | bytes 589828
  45.2 257.0 %all-reduce.3.cloned.1.call-start = ((), (), s32[]{:S(2)}) async-start(), calls=%async_computation.2 | async-start | bytes 393216 | tf_op jit(solution)/shard_map/psum | solution.py:38
  257.0 138.4 %all-gather.2.cloned.1.call-start = ((), (), s32[]{:S(2)}) async-start(), calls=%async_computation.3 | async-start | bytes 3342336 | tf_op jit(solution)/shard_map/all_gather | solution.py:45
  304.0 696.6 %all-reduce.5.cloned.1.call-start = ((), (), s32[]{:S(2)}) async-start(), calls=%async_computation.4 | async-start | bytes 393216 | tf_op jit(solution)/shard_map/psum | solution.py:43
  304.0 24.7 %copy-start.2 = (bf16[384,256]{1,0:T(8,128)(2,1)S(1)}, bf16[384,256]{1,0:T(8,128)(2,1)}, u32[]{:S(2)}) copy-start(bf16[384,256]{1,0:T(8,128)(2,1)} %get-tuple-element.3) | copy-start | bytes 589828
  304.0 24.7 %copy-start.3 = (bf16[384,192]{1,0:T(8,128)(2,1)S(1)}, bf16[384,192]{1,0:T(8,128)(2,1)}, u32[]{:S(2)}) copy-start(bf16[384,192]{1,0:T(8,128)(2,1)} %reduce-scatter.7.cloned.1.call-done) | copy-start | bytes 442372
  329.7 719.8 %reduce-scatter.9.cloned.1.call-start = ((), (), s32[]{:S(2)}) async-start(), calls=%async_computation.6 | async-start | bytes 983040
  398.5 652.6 %copy-start.1 = (bf16[1536,192]{0,1:T(8,128)(2,1)S(1)}, bf16[1536,192]{0,1:T(8,128)(2,1)}, u32[]{:S(2)}) copy-start(bf16[1536,192]{0,1:T(8,128)(2,1)} %param.7) | copy-start | bytes 1769476
Sparse Core Ops, SparseCore 0:
  45.3 209.8 reduce-scatter.6
  258.6 43.4 all-reduce.2
  305.3 90.1 all-gather.1
  397.9 602.5 all-reduce.4
  1003.1 46.2 reduce-scatter.8
where the time goes:
time: 1060 us
  waiting for transfers between devices  959 us (90%)
  local copies, waits for them, and re-layouts  55.8 us (5%)
  matrix products  22.5 us (2%)
  between operations  14.6 us (1%)
    psum x1, waiting for transfers between devices, shards(): lax.psum(weight_part, ('row', 'col')) * (1.0 / math.sqrt(nodes_total))  591 us
    unnamed x7, waiting for transfers between devices  257 us
    all_gather x1, waiting for transfers between devices, shards(): lax.all_gather(hidden_grad, 'col', axis=0, tiled=True)  65.7 us
    psum x1, waiting for transfers between devices, shards(): lax.psum(hidden_part.astype(jnp.bfloat16), 'feat').astype(jnp.float32)  45 us
    dot_general x1, local copies, waits for them, and re-layouts, shards(): jnp.einsum('rcij,rif->cjf', dense, targets, preferred_element_type=jnp.fl...  24.7 us
  transfers between devices with their start and end apart: 5, of which 5 were waited for; matrix products, arithmetic and copies ran while one was open for 4% of the time, Pallas kernels for 0%

commit v1 on v0

v1 whole, which is shorter than its diff:
```python
import functools
import math

import jax
import jax.numpy as jnp
from jax import lax
from jax.experimental import pallas as pl
from jax.experimental.pallas import tpu as pltpu
from jax.sharding import PartitionSpec as P

MESH = pl.DeviceIdType.MESH
F32 = jnp.float32
BF16 = jnp.bfloat16


def far_first(n):
    return sorted(range(1, n), key=lambda k: (-min(k, n - k), k))


def kernel(
    n_row, n_z, slots, total_nodes,
    rows_s, cols_s, prev_r, last_r, prev_c, last_c,
    feat_hbm, w_ref, tiles_hbm, cot_hbm,
    act_out, fg_out, wg_out,
    x_v, tiles_v, cot_v,
    y_send, y_recv, y_buf, prod_f,
    s_buf, yh_recv, t_buf, z_recv, hg_buf, act_v,
    prod_b, b_send, b_recv, b_full,
    u_f32, u_send, u_recv, v_buf, wg_piece,
    in_sem, p1_s, p1_r, p2_s, p2_r, p3a_s, p3a_r, p3b_s, p3b_r,
    act_s, act_r, p4z_s, p4z_r, p4y_s, p4y_r, p5_s, p5_r, p6_s, p6_r,
    k1_s, k1_r, k2_s, k2_r, k3_s, k3_r,
):
    f = lax.axis_index("feat")
    r = lax.axis_index("row")
    c = lax.axis_index("col")
    y_low, b = f // 2, f % 2
    z, h = c // 2, c % 2
    a = (y_low + h) % 2
    n_g = 2 * n_row

    def feat_of(role, core):
        return ((role + h) % 2) * 2 + core

    def remote(src, dst, send, recv, device):
        return pltpu.make_async_remote_copy(
            src_ref=src, dst_ref=dst, send_sem=send, recv_sem=recv, device_id=device, device_id_type=MESH
        )

    feat_peers = [{"feat": (f + k) % 4} for k in range(1, 4)]

    def g_peer(k):
        g2 = (2 * r + a + k) % n_g
        return g2, {"feat": feat_of(g2 % 2, b), "row": g2 // 2}

    def u_peer(k):
        u2 = (2 * r + h + k) % n_g
        return u2, {"row": u2 // 2, "col": 2 * z + u2 % 2}

    def z_peer(k):
        return {"col": 2 * ((z + k) % n_z) + h}

    y_partner = {"feat": (f + 2) % 4, "col": c + 1 - 2 * h}

    node_dev = x_v.shape[0]
    in_x = pltpu.make_async_copy(
        feat_hbm.at[pl.ds(pl.multiple_of(r * node_dev, node_dev), node_dev)], x_v, in_sem.at[0])
    in_t = pltpu.make_async_copy(tiles_hbm.at[:, a], tiles_v, in_sem.at[1])
    in_c = pltpu.make_async_copy(
        cot_hbm.at[:, a, :, pl.ds(pl.multiple_of(b * 128, 128), 128)], cot_v, in_sem.at[2])
    in_x.start()
    in_t.start()
    in_c.start()

    barrier = pltpu.get_barrier_semaphore()
    peers = list(feat_peers)
    for k in range(1, n_row):
        peers.append({"row": (r + k) % n_row})
        peers.append({"feat": (f + 2) % 4, "row": (r + k) % n_row})
    peers += [z_peer(k) for k in range(1, n_z)]
    peers.append(y_partner)
    peers += [{"row": (r + k) % n_row, "col": c + 1 - 2 * h} for k in range(n_row)]
    for peer in peers:
        pl.semaphore_signal(barrier, inc=1, device_id=peer, device_id_type=MESH)

    in_x.wait()
    y_part = jnp.dot(x_v[...], w_ref[...], preferred_element_type=F32).astype(BF16)
    for q in range(2):
        for core in range(2):
            y_send[2 * q + core] = y_part[192 * q:192 * (q + 1), 128 * core:128 * (core + 1)].reshape(3, 64, 128)
    pl.semaphore_wait(barrier, len(peers))

    copies = []
    for k in range(1, 4):
        f2 = (f + k) % 4
        piece = ((f2 // 2 + h) % 2) * 2 + f2 % 2
        cp = remote(y_send.at[piece], y_recv.at[k - 1], p1_s.at[k - 1], p1_r.at[k - 1], feat_peers[k - 1])
        cp.start()
        copies.append(cp)
    total = y_send[2 * a + b].astype(F32)
    for k in range(3):
        copies[k].wait_recv()
        total = total + y_recv[k].astype(F32)
    g = 2 * r + a
    y_buf[pl.ds(3 * g, 3)] = total.astype(BF16)

    p2 = []
    for k in range(1, n_g):
        _, dev = g_peer(k)
        cp = remote(y_buf.at[pl.ds(3 * g, 3)], y_buf.at[pl.ds(3 * g, 3)], p2_s.at[k - 1], p2_r.at[k - 1], dev)
        cp.start()
        p2.append(cp)
    prod_f[slots] = jnp.zeros((64, 128), F32)
    prod_b[slots] = jnp.zeros((128, 128), F32)
    in_t.wait()
    for k in range(1, n_g):
        src = (g + n_g - k) % n_g
        remote(y_buf.at[pl.ds(3 * src, 3)], y_buf.at[pl.ds(3 * src, 3)], p2_s.at[k - 1], p2_r.at[k - 1],
               y_partner).wait_recv()

    def forward(s, _):
        block = y_buf[pl.ds(2 * cols_s[s], 2)].reshape(128, 128)
        prod_f[s] = jnp.dot(tiles_v[s], block, preferred_element_type=F32)
        return 0

    lax.fori_loop(0, slots, forward, 0, unroll=8)

    def chain_forward(s, _):
        prod_f[s] = prod_f[s] + prod_f[prev_r[s]]
        return 0

    lax.fori_loop(0, slots, chain_forward, 0, unroll=4)

    def fill(c2):
        for w in range(3):
            s_buf[c2, w] = prod_f[last_r[3 * c2 + w]].astype(BF16)

    offs = far_first(n_z) + [0]
    p3a = []
    for j, off in enumerate(offs):
        c2 = 2 * ((z + off) % n_z) + 1 - h
        fill(c2)
        cp = remote(s_buf.at[c2], yh_recv.at[j], p3a_s.at[j], p3a_r.at[j], y_partner)
        cp.start()
        p3a.append(cp)
    for j, off in enumerate(offs):
        fill(2 * ((z + off) % n_z) + h)
    p3b = []
    for j, off in enumerate(offs):
        c2 = 2 * ((z + off) % n_z) + h
        p3a[j].wait_recv()
        both = s_buf[c2].astype(F32) + yh_recv[j].astype(F32)
        if off:
            t_buf[j] = both.astype(BF16)
            cp = remote(t_buf.at[j], z_recv.at[j], p3b_s.at[j], p3b_r.at[j], z_peer(off))
            cp.start()
            p3b.append(cp)
        else:
            hidden = both
    for j in range(n_z - 1):
        p3b[j].wait_recv()
        hidden = hidden + z_recv[j].astype(F32)

    in_c.wait()
    sigma = jax.nn.sigmoid(hidden)
    grad = cot_v[...].astype(F32) * (sigma * (1.0 + hidden * (1.0 - sigma)))
    hg_buf[pl.ds(3 * c, 3)] = grad.astype(BF16)
    act_v[...] = (hidden * sigma).astype(BF16)

    own = hg_buf.at[pl.ds(3 * c, 3)]
    p4y = [remote(own, own, p4y_s.at[n_z - 1], p4y_r.at[n_z - 1], y_partner)]
    p4y[0].start()
    p4z = []
    for j, off in enumerate(offs[:-1]):
        cp = remote(own, own, p4z_s.at[j], p4z_r.at[j], z_peer(off))
        cp.start()
        p4z.append(cp)
    act_cols = pl.ds(pl.multiple_of(b * 128, 128), 128)
    act_dst = act_out.at[:, a, :, act_cols]
    local = pltpu.make_async_copy(act_v, act_dst, in_sem.at[3])
    local.start()
    acts = []
    for k in range(1, 4):
        cp = remote(act_v, act_dst, act_s.at[k - 1], act_r.at[k - 1], feat_peers[k - 1])
        cp.start()
        acts.append(cp)
    for j in reversed(range(n_z - 1)):
        c2 = 2 * ((z + n_z - offs[j]) % n_z) + h
        got = hg_buf.at[pl.ds(3 * c2, 3)]
        remote(got, got, p4z_s.at[j], p4z_r.at[j], y_partner).wait_recv()
        cp = remote(got, got, p4y_s.at[j], p4y_r.at[j], y_partner)
        cp.start()
        p4y.append(cp)
    for j in range(n_z):
        off = offs[j]
        c2 = 2 * ((z + n_z - off) % n_z) + 1 - h
        got = hg_buf.at[pl.ds(3 * c2, 3)]
        remote(got, got, p4y_s.at[j], p4y_r.at[j], y_partner).wait_recv()

    def backward(s, _):
        prod_b[s] = lax.dot_general(
            tiles_v[s], hg_buf[rows_s[s]], (((0,), (0,)), ((), ())), preferred_element_type=F32)
        return 0

    lax.fori_loop(0, slots, backward, 0, unroll=8)

    def chain_backward(s, _):
        prod_b[s] = prod_b[s] + prod_b[prev_c[s]]
        return 0

    lax.fori_loop(0, slots, chain_backward, 0, unroll=4)

    for j in range(3 * n_row):
        b_send[pl.ds(2 * j, 2)] = prod_b[last_c[j]].astype(BF16).reshape(2, 64, 128)

    p5 = []
    for k in range(1, n_g):
        g2, dev = g_peer(k)
        cp = remote(b_send.at[pl.ds(3 * g2, 3)], b_recv.at[k - 1], p5_s.at[k - 1], p5_r.at[k - 1], dev)
        cp.start()
        p5.append(cp)
    total = b_send[pl.ds(3 * g, 3)].astype(F32)
    for k in range(n_g - 1):
        p5[k].wait_recv()
        total = total + b_recv[k].astype(F32)
    b_full[2 * a + b] = total.astype(BF16)

    mine = b_full.at[2 * a + b]
    p6 = []
    for k in range(1, 4):
        cp = remote(mine, mine, p6_s.at[k - 1], p6_r.at[k - 1], feat_peers[k - 1])
        cp.start()
        p6.append(cp)
    for k in range(1, 4):
        f2 = (f + 4 - k) % 4
        got = b_full.at[((f2 // 2 + h) % 2) * 2 + f2 % 2]
        remote(got, got, p6_s.at[k - 1], p6_r.at[k - 1], y_partner).wait_recv()

    piece_rows = u_f32.shape[1]
    for core in range(2):
        part = jnp.zeros((192, 128), F32)
        for q in range(2):
            part = part + lax.dot_general(
                x_v[192 * q:192 * (q + 1)], b_full[2 * q + core].reshape(192, 128),
                (((0,), (0,)), ((), ())), preferred_element_type=F32)
        part = part.reshape(n_row, piece_rows, 128)
        u_f32[n_row * core:n_row * (core + 1)] = part
        u_send[n_row * core:n_row * (core + 1)] = part.astype(BF16)
    u = 2 * r + h
    k1 = []
    for k in range(1, n_g):
        u2, dev = u_peer(k)
        cp = remote(u_send.at[u2], u_recv.at[k - 1], k1_s.at[k - 1], k1_r.at[k - 1], dev)
        cp.start()
        k1.append(cp)
    for q in range(2):
        grad_rows = jnp.zeros((192, w_ref.shape[0]), F32)
        for core in range(2):
            grad_rows = grad_rows + lax.dot_general(
                b_full[2 * q + core].reshape(192, 128), w_ref[:, 128 * core:128 * (core + 1)],
                (((1,), (1,)), ((), ())), preferred_element_type=F32)
        fg_out[192 * q:192 * (q + 1)] = grad_rows.astype(BF16)
    total = u_f32[u]
    for k in range(n_g - 1):
        k1[k].wait_recv()
        total = total + u_recv[k].astype(F32)
    v_buf[z] = total.astype(BF16)
    k2 = []
    for j, off in enumerate(offs[:-1]):
        cp = remote(v_buf.at[z], v_buf.at[z], k2_s.at[j], k2_r.at[j], z_peer(off))
        cp.start()
        k2.append(cp)
    for j, off in enumerate(offs[:-1]):
        got = v_buf.at[(z + n_z - off) % n_z]
        remote(got, got, k2_s.at[j], k2_r.at[j], y_partner).wait_recv()
    total = v_buf[0].astype(F32)
    for j in range(1, n_z):
        total = total + v_buf[j].astype(F32)
    wg_piece[...] = total * (1.0 / math.sqrt(total_nodes))

    def wg_place(piece):
        return wg_out.at[
            pl.ds(pl.multiple_of((piece % n_row) * piece_rows, piece_rows), piece_rows),
            pl.ds(pl.multiple_of((piece // n_row) * 128, 128), 128),
        ]

    local_wg = pltpu.make_async_copy(wg_piece, wg_place(u), in_sem.at[4])
    local_wg.start()
    k3 = []
    for k in range(1, n_g):
        _, dev = u_peer(k)
        cp = remote(wg_piece, wg_place(u), k3_s.at[k - 1], k3_r.at[k - 1], dev)
        cp.start()
        k3.append(cp)
    for k in range(1, n_g):
        got = wg_place((u + n_g - k) % n_g)
        remote(wg_piece, got, k3_s.at[k - 1], k3_r.at[k - 1], y_partner).wait_recv()
    for k in range(1, 4):
        f2 = (f + 4 - k) % 4
        got = act_out.at[:, (f2 // 2 + h) % 2, :, pl.ds(pl.multiple_of((f2 % 2) * 128, 128), 128)]
        remote(act_v, got, act_s.at[k - 1], act_r.at[k - 1], y_partner).wait_recv()
    local.wait()
    local_wg.wait()
    for cp in copies + p2 + p3a + p3b + p4y + p4z + acts + p5 + p6 + k1 + k2 + k3:
        cp.wait_send()


def slot_links(keys, count, places):
    slots = keys.shape[0]
    ids = jnp.arange(slots, dtype=jnp.int32)
    live = ids < count
    same = (keys[:, None] == keys[None, :]) & live[None, :] & (ids[None, :] < ids[:, None])
    prev = jnp.max(jnp.where(same, ids[None, :], -1), axis=1)
    there = (jnp.arange(places, dtype=jnp.int32)[:, None] == keys[None, :]) & live[None, :]
    last = jnp.max(jnp.where(there, ids[None, :], -1), axis=1)
    return jnp.where(prev < 0, slots, prev), jnp.where(last < 0, slots, last)


def shards(n_row, n_z, features, weight, tile_values, tile_rows, tile_cols, tile_count, cotangent):
    slots = tile_values.shape[2]
    node_dev, out = cotangent.shape
    width = features.shape[1]
    n_g = 2 * n_row
    n_col = 2 * n_z
    rows = tile_rows[0, 0]
    cols = tile_cols[0, 0]
    count = tile_count[0, 0]
    prev_r, last_r = slot_links(rows, count, 3 * n_col)
    prev_c, last_c = slot_links(cols, count, 3 * n_row)
    piece_rows = 2 * width // n_g
    dma = pltpu.SemaphoreType.DMA
    smem = pl.BlockSpec(memory_space=pltpu.SMEM)
    vmem = pl.BlockSpec(memory_space=pltpu.VMEM)
    hbm = pl.BlockSpec(memory_space=pl.ANY)
    sem_counts = [5, 3, 3, n_g - 1, n_g - 1, n_z, n_z, n_z - 1, n_z - 1, 3, 3, n_z - 1, n_z - 1, n_z, n_z,
                  n_g - 1, n_g - 1, 3, 3, n_g - 1, n_g - 1, n_z - 1, n_z - 1, n_g - 1, n_g - 1]
    act, fg, wg = pl.pallas_call(
        functools.partial(kernel, n_row, n_z, slots, node_dev * n_row * n_col),
        out_shape=[
            jax.ShapeDtypeStruct((3, 2, 64, out), BF16),
            jax.ShapeDtypeStruct((node_dev, width), BF16),
            jax.ShapeDtypeStruct((width, out), F32),
        ],
        in_specs=[smem] * 6 + [hbm, vmem, hbm, hbm],
        out_specs=[vmem] * 3,
        scratch_shapes=[
            pltpu.VMEM((node_dev, width), BF16),
            pltpu.VMEM((slots, 64, 128), BF16),
            pltpu.VMEM((3, 64, 128), BF16),
            pltpu.VMEM((4, 3, 64, 128), BF16),
            pltpu.VMEM((3, 3, 64, 128), BF16),
            pltpu.VMEM((3 * n_g, 64, 128), BF16),
            pltpu.VMEM((slots + 1, 64, 128), F32),
            pltpu.VMEM((n_col, 3, 64, 128), BF16),
            pltpu.VMEM((n_z, 3, 64, 128), BF16),
            pltpu.VMEM((n_z - 1, 3, 64, 128), BF16),
            pltpu.VMEM((n_z - 1, 3, 64, 128), BF16),
            pltpu.VMEM((3 * n_col, 64, 128), BF16),
            pltpu.VMEM((3, 64, 128), BF16),
            pltpu.VMEM((slots + 1, 128, 128), F32),
            pltpu.VMEM((3 * n_g, 64, 128), BF16),
            pltpu.VMEM((n_g - 1, 3, 64, 128), BF16),
            pltpu.VMEM((4, 3, 64, 128), BF16),
            pltpu.VMEM((n_g, piece_rows, 128), F32),
            pltpu.VMEM((n_g, piece_rows, 128), BF16),
            pltpu.VMEM((n_g - 1, piece_rows, 128), BF16),
            pltpu.VMEM((n_z, piece_rows, 128), BF16),
            pltpu.VMEM((piece_rows, 128), F32),
        ] + [dma((n,)) for n in sem_counts],
        compiler_params=pltpu.CompilerParams(
            collective_id=0, has_side_effects=True, vmem_limit_bytes=40 * 1024 * 1024),
    )(
        rows, cols, prev_r, last_r, prev_c, last_c,
        features, weight, tile_values.reshape(slots, 2, 64, 128), cotangent.reshape(3, 2, 64, out),
    )
    return act.reshape(node_dev, out), fg.reshape(1, node_dev, width), wg


def solution(mesh):
    return jax.shard_map(
        functools.partial(shards, mesh.shape["row"], mesh.shape["col"] // 2),
        mesh=mesh,
        in_specs=(
            P("col", "feat"),
            P("feat", None),
            P("row", "col", None, None, None),
            P("row", "col", None),
            P("row", "col", None),
            P("row", "col"),
            P(("row", "col"), None),
        ),
        out_specs=(P(("row", "col"), None), P("col", "row", "feat"), P("feat", None)),
        check_vma=False,
    )
```

time: 1060 us -> 98.5 us (0.09)
  waiting for transfers between devices: 959 us -> 0 us
  Pallas kernels: 0 us -> 86.2 us
  local copies, waits for them, and re-layouts: 55.8 us -> 8.19 us
  matrix products: 22.5 us -> 0 us
  between operations: 14.6 us -> 1.33 us
    psum x2 -> x0, waiting for transfers between devices: 636 us -> none  [the longest x1 591 us: shards(): lax.psum(weight_part, ('row', 'col')) * (1.0 / math.sqrt(nodes_total))]
    unnamed x7 -> x0, waiting for transfers between devices: 257 us -> none
    pallas_call x0 -> x1, Pallas kernels: none -> 86.2 us  [shards(): pl.pallas_call(functools.partial(kernel, n_row, n_z, slots, node_dev * n_...]
    all_gather x1 -> x0, waiting for transfers between devices: 65.7 us -> none  [shards(): lax.all_gather(hidden_grad, 'col', axis=0, tiled=True)]
    dot_general x2 -> x0, local copies, waits for them, and re-layouts: 34.3 us -> none  [the longest x1 24.7 us: shards(): jnp.einsum('rcij,rif->cjf', dense, targets, preferred_element_type=jnp.fl...]
    dot_general x5 -> x0, matrix products: 22.5 us -> none  [the longest x1 10.3 us: shards(): jnp.einsum('rcij,rif->cjf', dense, targets, preferred_element_type=jnp.fl...]
  transfers between devices with their start and end apart: 5 -> 0, of which waited for: 5 -> 0; matrix products, arithmetic and copies ran while one was open for 4% -> 0% of each run, Pallas kernels for 0% -> 0%
where the time goes in v1:
time: 98.5 us; the launch traced here: 98.2 us
  Pallas kernels  86.2 us (88%)
  local copies, waits for them, and re-layouts  8.19 us (8%)
  other arithmetic  2.5 us (3%)
  between operations  1.33 us (1%)
    pallas_call x1, Pallas kernels, shards(): pl.pallas_call(functools.partial(kernel, n_row, n_z, slots, node_dev * n_...  86.2 us
    unnamed x14, local copies, waits for them, and re-layouts  8.19 us

profile of v1, /device:TPU:1, one launch (start us, length us, event | category | flops | bytes accessed | tf_op | source)
XLA Modules:
  0.0 98.2 jit_solution(18046191712913260175)
XLA Ops:
  1.3 0.8 select_reduce_fusion.2
  2.1 0.8 select_reduce_fusion.3
  2.9 0.9 select_reduce_fusion
  3.8 1.3 %copy.12.feat_hbm = bf16[1536,192]{1,0:T(8,128)(2,1)S(1)} copy(bf16[1536,192]{0,1:T(8,128)(2,1)} %param.7) | data formatting | bytes 1179648 | tf_op args[0]
  5.2 0.0 copy-start
  5.2 1.6 %copy-done = bf16[1,1,64,128,128]{4,3,2,1,0:T(8,128)(2,1)S(1)} copy-done((bf16[1,1,64,128,128]{4,3,2,1,0:T(8,128)(2,1)S(1)}, bf16[1,1,64,128,128]{4,3,2,1,0:T(8,128)(2,1)}, u32[]{:S(2)}) %copy-start) | copy-done | bytes 2097176
  6.7 0.0 copy-start.1
  6.7 0.9 copy-done.1
  7.7 0.0 copy-start.2
  7.7 0.9 copy-done.2
  8.6 0.0 copy-start.3
  8.6 0.7 copy-done.3
  9.2 0.0 copy-start.4
  9.2 0.7 copy-done.4
  9.9 86.2 %shard_map.94 = (bf16[3,2,64,256]{3,2,1,0:T(8,128)(2,1)S(1)}, bf16[384,192]{1,0:T(8,128)(2,1)S(1)}, f32[192,256]{1,0:T(8,128)S(1)}) custom-call(s32[64]{0:T(128)S(1)} %bitcast.14, s32[64]{0:T(128)S(1)} %bitcast.17, s32[64]{0:T(128)S(1)} %get-tuple-element.18.prev_r, s32[48]{0:T(128)S(1)} %compare_select_fusion.2.last_r, s32[64]{0:T(128)S(1)} %get-tuple-element.17.prev_c, ...), custom_call_target="tpu_custom_call" | custom-call | tf_op jit(solution)/shard_map/pallas_call | solution.py:337
  96.1 0.8 copy.13
  96.9 0.7 copy.17
  97.6 0.7 copy.18
  (4 shorter events, 0.0 us)
Async XLA Ops:
  5.2 1.6 %copy-start = (bf16[1,1,64,128,128]{4,3,2,1,0:T(8,128)(2,1)S(1)}, bf16[1,1,64,128,128]{4,3,2,1,0:T(8,128)(2,1)}, u32[]{:S(2)}) copy-start(bf16[1,1,64,128,128]{4,3,2,1,0:T(8,128)(2,1)} %param.9) | copy-start | bytes 6291460
  6.7 0.9 copy-start.1
  7.7 0.9 copy-start.2
  8.6 0.7 copy-start.3
  9.2 0.7 copy-start.4

commit v2 on v1

--- a/solution.py
+++ b/solution.py
@@ -19,10 +19,10 @@
 
 def kernel(
     n_row, n_z, slots, total_nodes,
-    rows_s, cols_s, prev_r, last_r, prev_c, last_c,
-    feat_hbm, w_ref, tiles_hbm, cot_hbm,
+    rows_hbm, cols_hbm, count_s, feat_hbm, w_hbm, tiles_hbm, cot_hbm,
     act_out, fg_out, wg_out,
-    x_v, tiles_v, cot_v,
+    rows_s, cols_s, keys_v, links_v, links_s,
+    x_v, w_ref, tiles_v, cot_v,
     y_send, y_recv, y_buf, prod_f,
     s_buf, yh_recv, t_buf, z_recv, hg_buf, act_v,
     prod_b, b_send, b_recv, b_full,
@@ -62,13 +62,23 @@
 
     y_partner = {"feat": (f + 2) % 4, "col": c + 1 - 2 * h}
 
-    node_dev = x_v.shape[0]
+    node_dev = x_v.shape[1]
     in_x = pltpu.make_async_copy(
-        feat_hbm.at[pl.ds(pl.multiple_of(r * node_dev, node_dev), node_dev)], x_v, in_sem.at[0])
+        feat_hbm.at[:, pl.ds(pl.multiple_of(r * node_dev, node_dev), node_dev)], x_v, in_sem.at[0])
+    in_w = pltpu.make_async_copy(w_hbm, w_ref, in_sem.at[5])
+    in_keys = [
+        pltpu.make_async_copy(rows_hbm, keys_v.at[0], in_sem.at[6]),
+        pltpu.make_async_copy(cols_hbm, keys_v.at[1], in_sem.at[7]),
+        pltpu.make_async_copy(rows_hbm, rows_s, in_sem.at[8]),
+        pltpu.make_async_copy(cols_hbm, cols_s, in_sem.at[9]),
+    ]
     in_t = pltpu.make_async_copy(tiles_hbm.at[:, a], tiles_v, in_sem.at[1])
     in_c = pltpu.make_async_copy(
         cot_hbm.at[:, a, :, pl.ds(pl.multiple_of(b * 128, 128), 128)], cot_v, in_sem.at[2])
     in_x.start()
+    in_w.start()
+    for cp in in_keys:
+        cp.start()
     in_t.start()
     in_c.start()
 
@@ -84,7 +94,9 @@
         pl.semaphore_signal(barrier, inc=1, device_id=peer, device_id_type=MESH)
 
     in_x.wait()
-    y_part = jnp.dot(x_v[...], w_ref[...], preferred_element_type=F32).astype(BF16)
+    in_w.wait()
+    y_part = lax.dot_general(
+        x_v[...], w_ref[...], (((0,), (0,)), ((), ())), preferred_element_type=F32).astype(BF16)
     for q in range(2):
         for core in range(2):
             y_send[2 * q + core] = y_part[192 * q:192 * (q + 1), 128 * core:128 * (core + 1)].reshape(3, 64, 128)
@@ -97,6 +109,23 @@
         cp = remote(y_send.at[piece], y_recv.at[k - 1], p1_s.at[k - 1], p1_r.at[k - 1], feat_peers[k - 1])
         cp.start()
         copies.append(cp)
+    for cp in in_keys:
+        cp.wait()
+    ids = lax.broadcasted_iota(jnp.int32, (slots, 128), 0)
+    lanes = lax.broadcasted_iota(jnp.int32, (slots, 128), 1)
+    live = ids < count_s[0, 0]
+    for i in range(2):
+        across = jnp.broadcast_to(keys_v[i], (slots, slots))
+        across = jnp.concatenate([across, jnp.zeros((slots, 128 - slots), jnp.int32)], axis=1)
+        down = jnp.sum(jnp.where(ids == lanes, across, 0), axis=1, keepdims=True)
+        down = jnp.broadcast_to(down, (slots, 128))
+        before = jnp.where(live & (ids < lanes) & (down == across), ids, -1)
+        there = jnp.where(live & (down == lanes), ids, -1)
+        for w, found in ((0, before), (1, there)):
+            top = jnp.max(found, axis=0, keepdims=True)
+            links_v[pl.ds(2 * i + w, 1), :] = jnp.where(top < 0, slots, top)
+    links = pltpu.make_async_copy(links_v, links_s, in_sem.at[10])
+    links.start()
     total = y_send[2 * a + b].astype(F32)
     for k in range(3):
         copies[k].wait_recv()
@@ -113,27 +142,28 @@
     prod_f[slots] = jnp.zeros((64, 128), F32)
     prod_b[slots] = jnp.zeros((128, 128), F32)
     in_t.wait()
+    links.wait()
     for k in range(1, n_g):
         src = (g + n_g - k) % n_g
         remote(y_buf.at[pl.ds(3 * src, 3)], y_buf.at[pl.ds(3 * src, 3)], p2_s.at[k - 1], p2_r.at[k - 1],
                y_partner).wait_recv()
 
     def forward(s, _):
-        block = y_buf[pl.ds(2 * cols_s[s], 2)].reshape(128, 128)
+        block = y_buf[pl.ds(2 * cols_s[0, s], 2)].reshape(128, 128)
         prod_f[s] = jnp.dot(tiles_v[s], block, preferred_element_type=F32)
         return 0
 
     lax.fori_loop(0, slots, forward, 0, unroll=8)
 
     def chain_forward(s, _):
-        prod_f[s] = prod_f[s] + prod_f[prev_r[s]]
+        prod_f[s] = prod_f[s] + prod_f[links_s[0, s]]
         return 0
 
     lax.fori_loop(0, slots, chain_forward, 0, unroll=4)
 
     def fill(c2):
         for w in range(3):
-            s_buf[c2, w] = prod_f[last_r[3 * c2 + w]].astype(BF16)
+            s_buf[c2, w] = prod_f[links_s[1, 3 * c2 + w]].astype(BF16)
 
     offs = far_first(n_z) + [0]
     p3a = []
@@ -199,19 +229,19 @@
 
     def backward(s, _):
         prod_b[s] = lax.dot_general(
-            tiles_v[s], hg_buf[rows_s[s]], (((0,), (0,)), ((), ())), preferred_element_type=F32)
+            tiles_v[s], hg_buf[rows_s[0, s]], (((0,), (0,)), ((), ())), preferred_element_type=F32)
         return 0
 
     lax.fori_loop(0, slots, backward, 0, unroll=8)
 
     def chain_backward(s, _):
-        prod_b[s] = prod_b[s] + prod_b[prev_c[s]]
+        prod_b[s] = prod_b[s] + prod_b[links_s[2, s]]
         return 0
 
     lax.fori_loop(0, slots, chain_backward, 0, unroll=4)
 
     for j in range(3 * n_row):
-        b_send[pl.ds(2 * j, 2)] = prod_b[last_c[j]].astype(BF16).reshape(2, 64, 128)
+        b_send[pl.ds(2 * j, 2)] = prod_b[links_s[3, j]].astype(BF16).reshape(2, 64, 128)
 
     p5 = []
     for k in range(1, n_g):
@@ -223,9 +253,9 @@
     for k in range(n_g - 1):
         p5[k].wait_recv()
         total = total + b_recv[k].astype(F32)
-    b_full[2 * a + b] = total.astype(BF16)
-
-    mine = b_full.at[2 * a + b]
+    b_full[2 * b + a] = total.astype(BF16)
+
+    mine = b_full.at[2 * b + a]
     p6 = []
     for k in range(1, 4):
         cp = remote(mine, mine, p6_s.at[k - 1], p6_r.at[k - 1], feat_peers[k - 1])
@@ -233,16 +263,13 @@
         p6.append(cp)
     for k in range(1, 4):
         f2 = (f + 4 - k) % 4
-        got = b_full.at[((f2 // 2 + h) % 2) * 2 + f2 % 2]
+        got = b_full.at[2 * (f2 % 2) + (f2 // 2 + h) % 2]
         remote(got, got, p6_s.at[k - 1], p6_r.at[k - 1], y_partner).wait_recv()
 
     piece_rows = u_f32.shape[1]
     for core in range(2):
-        part = jnp.zeros((192, 128), F32)
-        for q in range(2):
-            part = part + lax.dot_general(
-                x_v[192 * q:192 * (q + 1)], b_full[2 * q + core].reshape(192, 128),
-                (((0,), (0,)), ((), ())), preferred_element_type=F32)
+        half = b_full[2 * core:2 * core + 2].reshape(node_dev, 128)
+        part = jnp.dot(x_v[...], half, preferred_element_type=F32)
         part = part.reshape(n_row, piece_rows, 128)
         u_f32[n_row * core:n_row * (core + 1)] = part
         u_send[n_row * core:n_row * (core + 1)] = part.astype(BF16)
@@ -253,13 +280,12 @@
         cp = remote(u_send.at[u2], u_recv.at[k - 1], k1_s.at[k - 1], k1_r.at[k - 1], dev)
         cp.start()
         k1.append(cp)
-    for q in range(2):
-        grad_rows = jnp.zeros((192, w_ref.shape[0]), F32)
-        for core in range(2):
-            grad_rows = grad_rows + lax.dot_general(
-                b_full[2 * q + core].reshape(192, 128), w_ref[:, 128 * core:128 * (core + 1)],
-                (((1,), (1,)), ((), ())), preferred_element_type=F32)
-        fg_out[192 * q:192 * (q + 1)] = grad_rows.astype(BF16)
+    grad_t = jnp.zeros((w_ref.shape[0], node_dev), F32)
+    for core in range(2):
+        grad_t = grad_t + lax.dot_general(
+            w_ref[:, 128 * core:128 * (core + 1)], b_full[2 * core:2 * core + 2].reshape(node_dev, 128),
+            (((1,), (1,)), ((), ())), preferred_element_type=F32)
+    fg_out[...] = grad_t.astype(BF16)
     total = u_f32[u]
     for k in range(n_g - 1):
         k1[k].wait_recv()
@@ -305,46 +331,36 @@
         cp.wait_send()
 
 
-def slot_links(keys, count, places):
-    slots = keys.shape[0]
-    ids = jnp.arange(slots, dtype=jnp.int32)
-    live = ids < count
-    same = (keys[:, None] == keys[None, :]) & live[None, :] & (ids[None, :] < ids[:, None])
-    prev = jnp.max(jnp.where(same, ids[None, :], -1), axis=1)
-    there = (jnp.arange(places, dtype=jnp.int32)[:, None] == keys[None, :]) & live[None, :]
-    last = jnp.max(jnp.where(there, ids[None, :], -1), axis=1)
-    return jnp.where(prev < 0, slots, prev), jnp.where(last < 0, slots, last)
-
-
 def shards(n_row, n_z, features, weight, tile_values, tile_rows, tile_cols, tile_count, cotangent):
     slots = tile_values.shape[2]
     node_dev, out = cotangent.shape
     width = features.shape[1]
     n_g = 2 * n_row
     n_col = 2 * n_z
-    rows = tile_rows[0, 0]
-    cols = tile_cols[0, 0]
-    count = tile_count[0, 0]
-    prev_r, last_r = slot_links(rows, count, 3 * n_col)
-    prev_c, last_c = slot_links(cols, count, 3 * n_row)
     piece_rows = 2 * width // n_g
     dma = pltpu.SemaphoreType.DMA
     smem = pl.BlockSpec(memory_space=pltpu.SMEM)
     vmem = pl.BlockSpec(memory_space=pltpu.VMEM)
-    hbm = pl.BlockSpec(memory_space=pl.ANY)
-    sem_counts = [5, 3, 3, n_g - 1, n_g - 1, n_z, n_z, n_z - 1, n_z - 1, 3, 3, n_z - 1, n_z - 1, n_z, n_z,
+    hbm = pl.BlockSpec(memory_space=pltpu.HBM)
+    sem_counts = [11, 3, 3, n_g - 1, n_g - 1, n_z, n_z, n_z - 1, n_z - 1, 3, 3, n_z - 1, n_z - 1, n_z, n_z,
                   n_g - 1, n_g - 1, 3, 3, n_g - 1, n_g - 1, n_z - 1, n_z - 1, n_g - 1, n_g - 1]
     act, fg, wg = pl.pallas_call(
         functools.partial(kernel, n_row, n_z, slots, node_dev * n_row * n_col),
         out_shape=[
             jax.ShapeDtypeStruct((3, 2, 64, out), BF16),
-            jax.ShapeDtypeStruct((node_dev, width), BF16),
+            jax.ShapeDtypeStruct((width, node_dev), BF16),
             jax.ShapeDtypeStruct((width, out), F32),
         ],
-        in_specs=[smem] * 6 + [hbm, vmem, hbm, hbm],
+        in_specs=[hbm, hbm, smem, hbm, hbm, hbm, hbm],
         out_specs=[vmem] * 3,
         scratch_shapes=[
-            pltpu.VMEM((node_dev, width), BF16),
+            pltpu.SMEM((1, slots), jnp.int32),
+            pltpu.SMEM((1, slots), jnp.int32),
+            pltpu.VMEM((2, 1, slots), jnp.int32),
+            pltpu.VMEM((8, 128), jnp.int32),
+            pltpu.SMEM((8, 128), jnp.int32),
+            pltpu.VMEM((width, node_dev), BF16),
+            pltpu.VMEM((width, out), BF16),
             pltpu.VMEM((slots, 64, 128), BF16),
             pltpu.VMEM((3, 64, 128), BF16),
             pltpu.VMEM((4, 3, 64, 128), BF16),
@@ -368,12 +384,12 @@
             pltpu.VMEM((piece_rows, 128), F32),
         ] + [dma((n,)) for n in sem_counts],
         compiler_params=pltpu.CompilerParams(
-            collective_id=0, has_side_effects=True, vmem_limit_bytes=40 * 1024 * 1024),
+            collective_id=0, has_side_effects=True, vmem_limit_bytes=60 * 1024 * 1024),
     )(
-        rows, cols, prev_r, last_r, prev_c, last_c,
-        features, weight, tile_values.reshape(slots, 2, 64, 128), cotangent.reshape(3, 2, 64, out),
+        tile_rows.reshape(1, slots), tile_cols.reshape(1, slots), tile_count,
+        features.T, weight, tile_values.reshape(slots, 2, 64, 128), cotangent.reshape(3, 2, 64, out),
     )
-    return act.reshape(node_dev, out), fg.reshape(1, node_dev, width), wg
+    return act.reshape(node_dev, out), fg.T.reshape(1, node_dev, width), wg
 
 
 def solution(mesh):

time: 98.5 us -> 93 us (0.944)
  local copies, waits for them, and re-layouts: 8.19 us -> 4.82 us
  other arithmetic: 2.5 us -> 0 us
    unnamed x14 -> x3, local copies, waits for them, and re-layouts: 8.19 us -> 4.82 us
    reduce_max x3 -> x0, other arithmetic: 2.48 us -> none  [the longest x2 1.55 us: slot_links(): last = jnp.max(jnp.where(there, ids[None, :], -1), axis=1)]
where the time goes in v2:
time: 93 us; the launch traced here: 92.8 us
  Pallas kernels  86.7 us (93%)
  local copies, waits for them, and re-layouts  4.82 us (5%)
  between operations  1.29 us (1%)
    pallas_call x1, Pallas kernels, shards(): pl.pallas_call(functools.partial(kernel, n_row, n_z, slots, node_dev * n_...  86.7 us
    unnamed x3, local copies, waits for them, and re-layouts  4.82 us

profile of v2, /device:TPU:1, one launch (start us, length us, event | category | flops | bytes accessed | tf_op | source)
XLA Modules:
  0.0 92.8 jit_solution(5727284011005295953)
XLA Ops:
  1.3 86.7 %shard_map.94 = (bf16[3,2,64,256]{3,2,1,0:T(8,128)(2,1)}, bf16[192,384]{1,0:T(8,128)(2,1)}, f32[192,256]{1,0:T(8,128)}) custom-call(s32[1,64]{1,0:T(1,128)} %bitcast.14, s32[1,64]{1,0:T(1,128)} %bitcast.15, s32[1,1]{1,0:T(1,128)S(6)} %copy.13.count_s, bf16[192,1536]{1,0:T(8,128)(2,1)} %bitcast.10, bf16[192,256]{1,0:T(8,128)(2,1)} %w_hbm.1, ...), custom_call_target="tpu_custom_call" | custom-call | tf_op jit(solution)/shard_map/pallas_call | solution.py:347
  88.0 1.6 %copy.14 = bf16[384,256]{1,0:T(8,128)(2,1)} copy(bf16[384,256]{1,0:T(8,128)(2,1)} %bitcast.12) | data formatting | bytes 393216
  89.6 1.6 %copy.15 = bf16[1,384,192]{1,2,0:T(8,128)(2,1)} copy(bf16[1,384,192]{1,2,0:T(8,128)(2,1)} %bitcast.13) | data formatting | bytes 294912
  91.2 1.6 %copy.16 = f32[192,256]{1,0:T(8,128)} copy(f32[192,256]{1,0:T(8,128)} %get-tuple-element.14) | data formatting | bytes 393216

commit v3 on v2

--- a/solution.py
+++ b/solution.py
@@ -25,10 +25,10 @@
     x_v, w_ref, tiles_v, cot_v,
     y_send, y_recv, y_buf, prod_f,
     s_buf, yh_recv, t_buf, z_recv, hg_buf, act_v,
-    prod_b, b_send, b_recv, b_full,
-    u_f32, u_send, u_recv, v_buf, wg_piece,
+    prod_b, b_both, b_recv, b_full,
+    xt_both, u_send, u_recv, v_buf, wg_piece,
     in_sem, p1_s, p1_r, p2_s, p2_r, p3a_s, p3a_r, p3b_s, p3b_r,
-    act_s, act_r, p4z_s, p4z_r, p4y_s, p4y_r, p5_s, p5_r, p6_s, p6_r,
+    act_s, act_r, p4z_s, p4z_r, p4y_s, p4y_r, xg_s, xg_r, bc_s, bc_r, p5_s, p5_r, p6_s, p6_r,
     k1_s, k1_r, k2_s, k2_r, k3_s, k3_r,
 ):
     f = lax.axis_index("feat")
@@ -81,6 +81,8 @@
         cp.start()
     in_t.start()
     in_c.start()
+    in_xt = pltpu.make_async_copy(feat_hbm, xt_both.at[y_low], in_sem.at[11])
+    in_xt.start()
 
     barrier = pltpu.get_barrier_semaphore()
     peers = list(feat_peers)
@@ -90,6 +92,7 @@
     peers += [z_peer(k) for k in range(1, n_z)]
     peers.append(y_partner)
     peers += [{"row": (r + k) % n_row, "col": c + 1 - 2 * h} for k in range(n_row)]
+    peers += [{"feat": (f + 2) % 4, "row": (r + k) % n_row, "col": c + 1 - 2 * h} for k in range(1, n_row)]
     for peer in peers:
         pl.semaphore_signal(barrier, inc=1, device_id=peer, device_id_type=MESH)
 
@@ -148,6 +151,9 @@
         remote(y_buf.at[pl.ds(3 * src, 3)], y_buf.at[pl.ds(3 * src, 3)], p2_s.at[k - 1], p2_r.at[k - 1],
                y_partner).wait_recv()
 
+    xg = remote(feat_hbm, xt_both.at[y_low], xg_s.at[0], xg_r.at[0], {"feat": (f + 2) % 4})
+    xg.start()
+
     def forward(s, _):
         block = y_buf[pl.ds(2 * cols_s[0, s], 2)].reshape(128, 128)
         prod_f[s] = jnp.dot(tiles_v[s], block, preferred_element_type=F32)
@@ -200,11 +206,40 @@
     own = hg_buf.at[pl.ds(3 * c, 3)]
     p4y = [remote(own, own, p4y_s.at[n_z - 1], p4y_r.at[n_z - 1], y_partner)]
     p4y[0].start()
+    def z_got(dist):
+        return hg_buf.at[pl.ds(3 * (2 * ((z + 2 * n_z - dist) % n_z) + h), 3)]
+
     p4z = []
-    for j, off in enumerate(offs[:-1]):
-        cp = remote(own, own, p4z_s.at[j], p4z_r.at[j], z_peer(off))
+
+    def z_send(what, j, off):
+        cp = remote(what, what, p4z_s.at[j], p4z_r.at[j], z_peer(off))
         cp.start()
         p4z.append(cp)
+
+    def arrived(j, dist):
+        got = z_got(dist)
+        remote(got, got, p4z_s.at[j], p4z_r.at[j], y_partner).wait_recv()
+        return got
+
+    def y_forward(got, j):
+        cp = remote(got, got, p4y_s.at[j], p4y_r.at[j], y_partner)
+        cp.start()
+        p4y.append(cp)
+
+    side = 1 - 2 * (z % 2)
+    z_send(own, 2, 2)
+    z_send(own, 3, n_z - 2)
+    z_send(own, 0, 1)
+    z_send(own, 1, n_z - 1)
+    y_forward(arrived(0, 1), 0)
+    y_forward(arrived(1, n_z - 1), 1)
+    plus = arrived(2, 2)
+    z_send(plus, 4, 1)
+    minus = arrived(3, n_z - 2)
+    z_send(minus, 5, n_z - 1)
+    z_send(hg_buf.at[pl.ds(3 * (2 * ((z + n_z - 2 * side) % n_z) + h), 3)], 6, 2 * side + n_z)
+    y_forward(plus, 2)
+    y_forward(minus, 3)
     act_cols = pl.ds(pl.multiple_of(b * 128, 128), 128)
     act_dst = act_out.at[:, a, :, act_cols]
     local = pltpu.make_async_copy(act_v, act_dst, in_sem.at[3])
@@ -214,17 +249,11 @@
         cp = remote(act_v, act_dst, act_s.at[k - 1], act_r.at[k - 1], feat_peers[k - 1])
         cp.start()
         acts.append(cp)
-    for j in reversed(range(n_z - 1)):
-        c2 = 2 * ((z + n_z - offs[j]) % n_z) + h
-        got = hg_buf.at[pl.ds(3 * c2, 3)]
-        remote(got, got, p4z_s.at[j], p4z_r.at[j], y_partner).wait_recv()
-        cp = remote(got, got, p4y_s.at[j], p4y_r.at[j], y_partner)
-        cp.start()
-        p4y.append(cp)
-    for j in range(n_z):
-        off = offs[j]
-        c2 = 2 * ((z + n_z - off) % n_z) + 1 - h
-        got = hg_buf.at[pl.ds(3 * c2, 3)]
+    y_forward(arrived(4, 3), 4)
+    y_forward(arrived(5, n_z - 3), 5)
+    y_forward(arrived(6, 4), 6)
+    for j, dist in enumerate([1, n_z - 1, 2, n_z - 2, 3, n_z - 3, 4, 0]):
+        got = hg_buf.at[pl.ds(3 * (2 * ((z + n_z - dist) % n_z) + 1 - h), 3)]
         remote(got, got, p4y_s.at[j], p4y_r.at[j], y_partner).wait_recv()
 
     def backward(s, _):
@@ -241,61 +270,73 @@
     lax.fori_loop(0, slots, chain_backward, 0, unroll=4)
 
     for j in range(3 * n_row):
-        b_send[pl.ds(2 * j, 2)] = prod_b[links_s[3, j]].astype(BF16).reshape(2, 64, 128)
+        b_both[b, pl.ds(2 * j, 2)] = prod_b[links_s[3, j]].astype(BF16).reshape(2, 64, 128)
+
+    bc = remote(b_both.at[b], b_both.at[b], bc_s.at[0], bc_r.at[0], {"feat": f + 1 - 2 * b})
+    bc.start()
 
     p5 = []
     for k in range(1, n_g):
         g2, dev = g_peer(k)
-        cp = remote(b_send.at[pl.ds(3 * g2, 3)], b_recv.at[k - 1], p5_s.at[k - 1], p5_r.at[k - 1], dev)
+        cp = remote(b_both.at[b, pl.ds(3 * g2, 3)], b_recv.at[k - 1], p5_s.at[k - 1], p5_r.at[k - 1], dev)
         cp.start()
         p5.append(cp)
-    total = b_send[pl.ds(3 * g, 3)].astype(F32)
+
+    piece_rows = u_send.shape[2]
+    in_xt.wait()
+    xg.wait_recv()
+    got = b_both.at[1 - b]
+    remote(got, got, bc_s.at[0], bc_r.at[0], y_partner).wait_recv()
+    both = jnp.concatenate([b_both[0].reshape(n_row * node_dev, 128), b_both[1].reshape(n_row * node_dev, 128)], axis=1)
+    for low in range(2):
+        part = jnp.dot(xt_both[low], both, preferred_element_type=F32).astype(BF16)
+        for core in range(2):
+            u_send[low, n_row * core:n_row * (core + 1)] = part[:, 128 * core:128 * (core + 1)].reshape(
+                n_row, piece_rows, 128)
+    u = 2 * r + h
+    k1 = []
+    for k in range(1, 2 * n_g):
+        q2 = (n_g * y_low + u + k) % (2 * n_g)
+        low2, u2 = q2 // n_g, q2 % n_g
+        dev = {"feat": 2 * low2 + b, "row": u2 // 2, "col": 2 * z + u2 % 2}
+        cp = remote(u_send.at[low2, u2], u_recv.at[k - 1], k1_s.at[k - 1], k1_r.at[k - 1], dev)
+        cp.start()
+        k1.append(cp)
+
+    total = b_both[b, pl.ds(3 * g, 3)].astype(F32)
     for k in range(n_g - 1):
         p5[k].wait_recv()
         total = total + b_recv[k].astype(F32)
     b_full[2 * b + a] = total.astype(BF16)
-
     mine = b_full.at[2 * b + a]
     p6 = []
     for k in range(1, 4):
         cp = remote(mine, mine, p6_s.at[k - 1], p6_r.at[k - 1], feat_peers[k - 1])
         cp.start()
         p6.append(cp)
+
+    total = u_send[y_low, u].astype(F32)
+    for k in range(2 * n_g - 1):
+        k1[k].wait_recv()
+        total = total + u_recv[k].astype(F32)
+    v_buf[z] = total.astype(BF16)
+    k2 = []
+    for j, off in enumerate(offs[:-1]):
+        cp = remote(v_buf.at[z], v_buf.at[z], k2_s.at[j], k2_r.at[j], z_peer(off))
+        cp.start()
+        k2.append(cp)
+
     for k in range(1, 4):
         f2 = (f + 4 - k) % 4
         got = b_full.at[2 * (f2 % 2) + (f2 // 2 + h) % 2]
         remote(got, got, p6_s.at[k - 1], p6_r.at[k - 1], y_partner).wait_recv()
-
-    piece_rows = u_f32.shape[1]
-    for core in range(2):
-        half = b_full[2 * core:2 * core + 2].reshape(node_dev, 128)
-        part = jnp.dot(x_v[...], half, preferred_element_type=F32)
-        part = part.reshape(n_row, piece_rows, 128)
-        u_f32[n_row * core:n_row * (core + 1)] = part
-        u_send[n_row * core:n_row * (core + 1)] = part.astype(BF16)
-    u = 2 * r + h
-    k1 = []
-    for k in range(1, n_g):
-        u2, dev = u_peer(k)
-        cp = remote(u_send.at[u2], u_recv.at[k - 1], k1_s.at[k - 1], k1_r.at[k - 1], dev)
-        cp.start()
-        k1.append(cp)
     grad_t = jnp.zeros((w_ref.shape[0], node_dev), F32)
     for core in range(2):
         grad_t = grad_t + lax.dot_general(
             w_ref[:, 128 * core:128 * (core + 1)], b_full[2 * core:2 * core + 2].reshape(node_dev, 128),
             (((1,), (1,)), ((), ())), preferred_element_type=F32)
     fg_out[...] = grad_t.astype(BF16)
-    total = u_f32[u]
-    for k in range(n_g - 1):
-        k1[k].wait_recv()
-        total = total + u_recv[k].astype(F32)
-    v_buf[z] = total.astype(BF16)
-    k2 = []
-    for j, off in enumerate(offs[:-1]):
-        cp = remote(v_buf.at[z], v_buf.at[z], k2_s.at[j], k2_r.at[j], z_peer(off))
-        cp.start()
-        k2.append(cp)
+
     for j, off in enumerate(offs[:-1]):
         got = v_buf.at[(z + n_z - off) % n_z]
         remote(got, got, k2_s.at[j], k2_r.at[j], y_partner).wait_recv()
@@ -327,7 +368,7 @@
         remote(act_v, got, act_s.at[k - 1], act_r.at[k - 1], y_partner).wait_recv()
     local.wait()
     local_wg.wait()
-    for cp in copies + p2 + p3a + p3b + p4y + p4z + acts + p5 + p6 + k1 + k2 + k3:
+    for cp in copies + p2 + p3a + p3b + p4y + p4z + acts + p5 + p6 + k1 + k2 + k3 + [xg, bc]:
         cp.wait_send()
 
 
@@ -342,8 +383,8 @@
     smem = pl.BlockSpec(memory_space=pltpu.SMEM)
     vmem = pl.BlockSpec(memory_space=pltpu.VMEM)
     hbm = pl.BlockSpec(memory_space=pltpu.HBM)
-    sem_counts = [11, 3, 3, n_g - 1, n_g - 1, n_z, n_z, n_z - 1, n_z - 1, 3, 3, n_z - 1, n_z - 1, n_z, n_z,
-                  n_g - 1, n_g - 1, 3, 3, n_g - 1, n_g - 1, n_z - 1, n_z - 1, n_g - 1, n_g - 1]
+    sem_counts = [12, 3, 3, n_g - 1, n_g - 1, n_z, n_z, n_z - 1, n_z - 1, 3, 3, n_z - 1, n_z - 1, n_z, n_z,
+                  1, 1, 1, 1, n_g - 1, n_g - 1, 3, 3, 2 * n_g - 1, 2 * n_g - 1, n_z - 1, n_z - 1, n_g - 1, n_g - 1]
     act, fg, wg = pl.pallas_call(
         functools.partial(kernel, n_row, n_z, slots, node_dev * n_row * n_col),
         out_shape=[
@@ -374,12 +415,12 @@
             pltpu.VMEM((3 * n_col, 64, 128), BF16),
             pltpu.VMEM((3, 64, 128), BF16),
             pltpu.VMEM((slots + 1, 128, 128), F32),
-            pltpu.VMEM((3 * n_g, 64, 128), BF16),
+            pltpu.VMEM((2, 3 * n_g, 64, 128), BF16),
             pltpu.VMEM((n_g - 1, 3, 64, 128), BF16),
             pltpu.VMEM((4, 3, 64, 128), BF16),
-            pltpu.VMEM((n_g, piece_rows, 128), F32),
-            pltpu.VMEM((n_g, piece_rows, 128), BF16),
-            pltpu.VMEM((n_g - 1, piece_rows, 128), BF16),
+            pltpu.VMEM((2, width, n_row * node_dev), BF16),
+            pltpu.VMEM((2, n_g, piece_rows, 128), BF16),
+            pltpu.VMEM((2 * n_g - 1, piece_rows, 128), BF16),
             pltpu.VMEM((n_z, piece_rows, 128), BF16),
             pltpu.VMEM((piece_rows, 128), F32),
         ] + [dma((n,)) for n in sem_counts],

time: 93 us -> 81.4 us (0.88)
  the two profiles are of different devices: /device:TPU:1 before, /device:TPU:8 now
where the time goes in v3:
time: 81.4 us; the launch traced here: 81.2 us
  Pallas kernels  75.1 us (92%)
  local copies, waits for them, and re-layouts  4.82 us (6%)
  between operations  1.29 us (2%)
    pallas_call x1, Pallas kernels, shards(): pl.pallas_call(functools.partial(kernel, n_row, n_z, slots, node_dev * n_...  75.1 us
    unnamed x3, local copies, waits for them, and re-layouts  4.82 us

profile of v3, /device:TPU:8, one launch (start us, length us, event | category | flops | bytes accessed | tf_op | source)
XLA Modules:
  0.0 81.2 jit_solution(731315542849941300)
XLA Ops:
  1.3 75.1 %shard_map.94 = (bf16[3,2,64,256]{3,2,1,0:T(8,128)(2,1)}, bf16[192,384]{1,0:T(8,128)(2,1)}, f32[192,256]{1,0:T(8,128)}) custom-call(s32[1,64]{1,0:T(1,128)} %bitcast.14, s32[1,64]{1,0:T(1,128)} %bitcast.15, s32[1,1]{1,0:T(1,128)S(6)} %copy.13.count_s, bf16[192,1536]{1,0:T(8,128)(2,1)} %bitcast.10, bf16[192,256]{1,0:T(8,128)(2,1)} %w_hbm.1, ...), custom_call_target="tpu_custom_call" | custom-call | tf_op jit(solution)/shard_map/pallas_call | solution.py:388
  76.4 1.6 %copy.14 = bf16[384,256]{1,0:T(8,128)(2,1)} copy(bf16[384,256]{1,0:T(8,128)(2,1)} %bitcast.12) | data formatting | bytes 393216
  78.0 1.6 %copy.15 = bf16[1,384,192]{1,2,0:T(8,128)(2,1)} copy(bf16[1,384,192]{1,2,0:T(8,128)(2,1)} %bitcast.13) | data formatting | bytes 294912
  79.6 1.6 %copy.16 = f32[192,256]{1,0:T(8,128)} copy(f32[192,256]{1,0:T(8,128)} %get-tuple-element.14) | data formatting | bytes 393216

commit v4 on v3

--- a/solution.py
+++ b/solution.py
@@ -275,13 +275,6 @@
     bc = remote(b_both.at[b], b_both.at[b], bc_s.at[0], bc_r.at[0], {"feat": f + 1 - 2 * b})
     bc.start()
 
-    p5 = []
-    for k in range(1, n_g):
-        g2, dev = g_peer(k)
-        cp = remote(b_both.at[b, pl.ds(3 * g2, 3)], b_recv.at[k - 1], p5_s.at[k - 1], p5_r.at[k - 1], dev)
-        cp.start()
-        p5.append(cp)
-
     piece_rows = u_send.shape[2]
     in_xt.wait()
     xg.wait_recv()
@@ -303,6 +296,24 @@
         cp.start()
         k1.append(cp)
 
+    p5 = []
+    for k in range(1, n_g):
+        g2, dev = g_peer(k)
+        cp = remote(b_both.at[b, pl.ds(3 * g2, 3)], b_recv.at[k - 1], p5_s.at[k - 1], p5_r.at[k - 1], dev)
+        cp.start()
+        p5.append(cp)
+
+    total = u_send[y_low, u].astype(F32)
+    for k in range(2 * n_g - 1):
+        k1[k].wait_recv()
+        total = total + u_recv[k].astype(F32)
+    v_buf[z] = total.astype(BF16)
+    k2 = []
+    for j, off in enumerate(offs[:-1]):
+        cp = remote(v_buf.at[z], v_buf.at[z], k2_s.at[j], k2_r.at[j], z_peer(off))
+        cp.start()
+        k2.append(cp)
+
     total = b_both[b, pl.ds(3 * g, 3)].astype(F32)
     for k in range(n_g - 1):
         p5[k].wait_recv()
@@ -315,17 +326,28 @@
         cp.start()
         p6.append(cp)
 
-    total = u_send[y_low, u].astype(F32)
-    for k in range(2 * n_g - 1):
-        k1[k].wait_recv()
-        total = total + u_recv[k].astype(F32)
-    v_buf[z] = total.astype(BF16)
-    k2 = []
     for j, off in enumerate(offs[:-1]):
-        cp = remote(v_buf.at[z], v_buf.at[z], k2_s.at[j], k2_r.at[j], z_peer(off))
-        cp.start()
-        k2.append(cp)
-
+        got = v_buf.at[(z + n_z - off) % n_z]
+        remote(got, got, k2_s.at[j], k2_r.at[j], y_partner).wait_recv()
+    total = v_buf[0].astype(F32)
+    for j in range(1, n_z):
+        total = total + v_buf[j].astype(F32)
+    wg_piece[...] = total * (1.0 / math.sqrt(total_nodes))
+
+    def wg_place(piece):
+        return wg_out.at[
+            pl.ds(pl.multiple_of((piece % n_row) * piece_rows, piece_rows), piece_rows),
+            pl.ds(pl.multiple_of((piece // n_row) * 128, 128), 128),
+        ]
+
+    local_wg = pltpu.make_async_copy(wg_piece, wg_place(u), in_sem.at[4])
+    local_wg.start()
+    k3 = []
+    for k in range(1, n_g):
+        _, dev = u_peer(k)
+        cp = remote(wg_piece, wg_place(u), k3_s.at[k - 1], k3_r.at[k - 1], dev)
+        cp.start()
+        k3.append(cp)
     for k in range(1, 4):
         f2 = (f + 4 - k) % 4
         got = b_full.at[2 * (f2 % 2) + (f2 // 2 + h) % 2]
@@ -337,28 +359,6 @@
             (((1,), (1,)), ((), ())), preferred_element_type=F32)
     fg_out[...] = grad_t.astype(BF16)
 
-    for j, off in enumerate(offs[:-1]):
-        got = v_buf.at[(z + n_z - off) % n_z]
-        remote(got, got, k2_s.at[j], k2_r.at[j], y_partner).wait_recv()
-    total = v_buf[0].astype(F32)
-    for j in range(1, n_z):
-        total = total + v_buf[j].astype(F32)
-    wg_piece[...] = total * (1.0 / math.sqrt(total_nodes))
-
-    def wg_place(piece):
-        return wg_out.at[
-            pl.ds(pl.multiple_of((piece % n_row) * piece_rows, piece_rows), piece_rows),
-            pl.ds(pl.multiple_of((piece // n_row) * 128, 128), 128),
-        ]
-
-    local_wg = pltpu.make_async_copy(wg_piece, wg_place(u), in_sem.at[4])
-    local_wg.start()
-    k3 = []
-    for k in range(1, n_g):
-        _, dev = u_peer(k)
-        cp = remote(wg_piece, wg_place(u), k3_s.at[k - 1], k3_r.at[k - 1], dev)
-        cp.start()
-        k3.append(cp)
     for k in range(1, n_g):
         got = wg_place((u + n_g - k) % n_g)
         remote(wg_piece, got, k3_s.at[k - 1], k3_r.at[k - 1], y_partner).wait_recv()
@@ -380,6 +380,7 @@
     n_col = 2 * n_z
     piece_rows = 2 * width // n_g
     dma = pltpu.SemaphoreType.DMA
+    pin = lambda x: pltpu.with_memory_space_constraint(x, pltpu.HBM)
     smem = pl.BlockSpec(memory_space=pltpu.SMEM)
     vmem = pl.BlockSpec(memory_space=pltpu.VMEM)
     hbm = pl.BlockSpec(memory_space=pltpu.HBM)
@@ -425,10 +426,10 @@
             pltpu.VMEM((piece_rows, 128), F32),
         ] + [dma((n,)) for n in sem_counts],
         compiler_params=pltpu.CompilerParams(
-            collective_id=0, has_side_effects=True, vmem_limit_bytes=60 * 1024 * 1024),
+            collective_id=0, has_side_effects=True, vmem_limit_bytes=40 * 1024 * 1024),
     )(
-        tile_rows.reshape(1, slots), tile_cols.reshape(1, slots), tile_count,
-        features.T, weight, tile_values.reshape(slots, 2, 64, 128), cotangent.reshape(3, 2, 64, out),
+        pin(tile_rows.reshape(1, slots)), pin(tile_cols.reshape(1, slots)), tile_count,
+        pin(features.T), pin(weight), pin(tile_values.reshape(slots, 2, 64, 128)), pin(cotangent.reshape(3, 2, 64, out)),
     )
     return act.reshape(node_dev, out), fg.T.reshape(1, node_dev, width), wg
 

time: 81.4 us -> 77.7 us (0.955)
  the two profiles are of different devices: /device:TPU:8 before, /device:TPU:1 now
where the time goes in v4:
time: 77.7 us; the launch traced here: 77.6 us
  Pallas kernels  74.3 us (96%)
  local copies, waits for them, and re-layouts  2.02 us (3%)
  between operations  1.29 us (2%)
    pallas_call x1, Pallas kernels, shards(): pl.pallas_call(functools.partial(kernel, n_row, n_z, slots, node_dev * n_...  74.3 us
    unnamed x3, local copies, waits for them, and re-layouts  2.02 us

profile of v4, /device:TPU:1, one launch (start us, length us, event | category | flops | bytes accessed | tf_op | source)
XLA Modules:
  0.0 77.6 jit_solution(4249604202625852731)
XLA Ops:
  1.3 74.3 %shard_map.94 = (bf16[3,2,64,256]{3,2,1,0:T(8,128)(2,1)S(1)}, bf16[192,384]{1,0:T(8,128)(2,1)S(1)}, f32[192,256]{1,0:T(8,128)S(1)}) custom-call(s32[1,64]{1,0:T(1,128)} %bitcast.14, s32[1,64]{1,0:T(1,128)} %bitcast.15, s32[1,1]{1,0:T(1,128)S(6)} %copy.13.count_s, bf16[192,1536]{1,0:T(8,128)(2,1)} %bitcast.12, bf16[192,256]{1,0:T(8,128)(2,1)} %w_hbm.1, ...), custom_call_target="tpu_custom_call" | custom-call | tf_op jit(solution)/shard_map/pallas_call | solution.py:389
  75.6 0.7 copy.14
  76.3 0.7 copy.15
  76.9 0.7 copy.16

commit v5 on v4

--- a/solution.py
+++ b/solution.py
@@ -77,12 +77,6 @@
         cot_hbm.at[:, a, :, pl.ds(pl.multiple_of(b * 128, 128), 128)], cot_v, in_sem.at[2])
     in_x.start()
     in_w.start()
-    for cp in in_keys:
-        cp.start()
-    in_t.start()
-    in_c.start()
-    in_xt = pltpu.make_async_copy(feat_hbm, xt_both.at[y_low], in_sem.at[11])
-    in_xt.start()
 
     barrier = pltpu.get_barrier_semaphore()
     peers = list(feat_peers)
@@ -93,8 +87,14 @@
     peers.append(y_partner)
     peers += [{"row": (r + k) % n_row, "col": c + 1 - 2 * h} for k in range(n_row)]
     peers += [{"feat": (f + 2) % 4, "row": (r + k) % n_row, "col": c + 1 - 2 * h} for k in range(1, n_row)]
-    for peer in peers:
+    for peer in reversed(peers):
         pl.semaphore_signal(barrier, inc=1, device_id=peer, device_id_type=MESH)
+    for cp in in_keys:
+        cp.start()
+    in_t.start()
+    in_c.start()
+    in_xt = pltpu.make_async_copy(feat_hbm, xt_both.at[y_low], in_sem.at[11])
+    in_xt.start()
 
     in_x.wait()
     in_w.wait()
@@ -156,16 +156,10 @@
 
     def forward(s, _):
         block = y_buf[pl.ds(2 * cols_s[0, s], 2)].reshape(128, 128)
-        prod_f[s] = jnp.dot(tiles_v[s], block, preferred_element_type=F32)
+        prod_f[s] = jnp.dot(tiles_v[s], block, preferred_element_type=F32) + prod_f[links_s[0, s]]
         return 0
 
-    lax.fori_loop(0, slots, forward, 0, unroll=8)
-
-    def chain_forward(s, _):
-        prod_f[s] = prod_f[s] + prod_f[links_s[0, s]]
-        return 0
-
-    lax.fori_loop(0, slots, chain_forward, 0, unroll=4)
+    lax.fori_loop(0, slots, forward, 0, unroll=32)
 
     def fill(c2):
         for w in range(3):
@@ -258,16 +252,10 @@
 
     def backward(s, _):
         prod_b[s] = lax.dot_general(
-            tiles_v[s], hg_buf[rows_s[0, s]], (((0,), (0,)), ((), ())), preferred_element_type=F32)
+            tiles_v[s], hg_buf[rows_s[0, s]], (((0,), (0,)), ((), ())), preferred_element_type=F32) + prod_b[links_s[2, s]]
         return 0
 
-    lax.fori_loop(0, slots, backward, 0, unroll=8)
-
-    def chain_backward(s, _):
-        prod_b[s] = prod_b[s] + prod_b[links_s[2, s]]
-        return 0
-
-    lax.fori_loop(0, slots, chain_backward, 0, unroll=4)
+    lax.fori_loop(0, slots, backward, 0, unroll=32)
 
     for j in range(3 * n_row):
         b_both[b, pl.ds(2 * j, 2)] = prod_b[links_s[3, j]].astype(BF16).reshape(2, 64, 128)

time: 77.7 us -> 74.4 us (0.958)
  Pallas kernels: 74.3 us -> 71 us
    pallas_call x1, Pallas kernels: 74.3 us -> 71 us  [shards(): pl.pallas_call(functools.partial(kernel, n_row, n_z, slots, node_dev * n_...]
where the time goes in v5:
time: 74.4 us; the launch traced here: 74.3 us
  Pallas kernels  71 us (95%)
  local copies, waits for them, and re-layouts  2.02 us (3%)
  between operations  1.29 us (2%)
    pallas_call x1, Pallas kernels, shards(): pl.pallas_call(functools.partial(kernel, n_row, n_z, slots, node_dev * n_...  71 us
    unnamed x3, local copies, waits for them, and re-layouts  2.02 us

profile of v5, /device:TPU:1, one launch (start us, length us, event | category | flops | bytes accessed | tf_op | source)
XLA Modules:
  0.0 74.3 jit_solution(10643218434379246820)
XLA Ops:
  1.3 71.0 %shard_map.94 = (bf16[3,2,64,256]{3,2,1,0:T(8,128)(2,1)S(1)}, bf16[192,384]{1,0:T(8,128)(2,1)S(1)}, f32[192,256]{1,0:T(8,128)S(1)}) custom-call(s32[1,64]{1,0:T(1,128)} %bitcast.14, s32[1,64]{1,0:T(1,128)} %bitcast.15, s32[1,1]{1,0:T(1,128)S(6)} %copy.13.count_s, bf16[192,1536]{1,0:T(8,128)(2,1)} %bitcast.12, bf16[192,256]{1,0:T(8,128)(2,1)} %w_hbm.1, ...), custom_call_target="tpu_custom_call" | custom-call | tf_op jit(solution)/shard_map/pallas_call | solution.py:377
  72.3 0.7 copy.14
  72.9 0.7 copy.15
  73.6 0.7 copy.16

commit v6 on v5

--- a/solution.py
+++ b/solution.py
@@ -106,12 +106,15 @@
     pl.semaphore_wait(barrier, len(peers))
 
     copies = []
-    for k in range(1, 4):
-        f2 = (f + k) % 4
-        piece = ((f2 // 2 + h) % 2) * 2 + f2 % 2
-        cp = remote(y_send.at[piece], y_recv.at[k - 1], p1_s.at[k - 1], p1_r.at[k - 1], feat_peers[k - 1])
-        cp.start()
-        copies.append(cp)
+    p1 = [[], [], []]
+    for w in range(3):
+        for k in range(1, 4):
+            f2 = (f + k) % 4
+            piece = ((f2 // 2 + h) % 2) * 2 + f2 % 2
+            cp = remote(y_send.at[piece, w], y_recv.at[k - 1, w], p1_s.at[k - 1, w], p1_r.at[k - 1, w], feat_peers[k - 1])
+            cp.start()
+            copies.append(cp)
+            p1[w].append(cp)
     for cp in in_keys:
         cp.wait()
     ids = lax.broadcasted_iota(jnp.int32, (slots, 128), 0)
@@ -129,27 +132,28 @@
             links_v[pl.ds(2 * i + w, 1), :] = jnp.where(top < 0, slots, top)
     links = pltpu.make_async_copy(links_v, links_s, in_sem.at[10])
     links.start()
-    total = y_send[2 * a + b].astype(F32)
-    for k in range(3):
-        copies[k].wait_recv()
-        total = total + y_recv[k].astype(F32)
     g = 2 * r + a
-    y_buf[pl.ds(3 * g, 3)] = total.astype(BF16)
-
     p2 = []
-    for k in range(1, n_g):
-        _, dev = g_peer(k)
-        cp = remote(y_buf.at[pl.ds(3 * g, 3)], y_buf.at[pl.ds(3 * g, 3)], p2_s.at[k - 1], p2_r.at[k - 1], dev)
-        cp.start()
-        p2.append(cp)
+    for w in range(3):
+        total = y_send[2 * a + b, w].astype(F32)
+        for k in range(3):
+            p1[w][k].wait_recv()
+            total = total + y_recv[k, w].astype(F32)
+        y_buf[3 * g + w] = total.astype(BF16)
+        mine = y_buf.at[3 * g + w]
+        for k in range(1, n_g):
+            _, dev = g_peer(k)
+            cp = remote(mine, mine, p2_s.at[k - 1, w], p2_r.at[k - 1, w], dev)
+            cp.start()
+            p2.append(cp)
     prod_f[slots] = jnp.zeros((64, 128), F32)
     prod_b[slots] = jnp.zeros((128, 128), F32)
     in_t.wait()
     links.wait()
-    for k in range(1, n_g):
-        src = (g + n_g - k) % n_g
-        remote(y_buf.at[pl.ds(3 * src, 3)], y_buf.at[pl.ds(3 * src, 3)], p2_s.at[k - 1], p2_r.at[k - 1],
-               y_partner).wait_recv()
+    for w in range(3):
+        for k in range(1, n_g):
+            got = y_buf.at[3 * ((g + n_g - k) % n_g) + w]
+            remote(got, got, p2_s.at[k - 1, w], p2_r.at[k - 1, w], y_partner).wait_recv()
 
     xg = remote(feat_hbm, xt_both.at[y_low], xg_s.at[0], xg_r.at[0], {"feat": (f + 2) % 4})
     xg.start()
@@ -161,94 +165,123 @@
 
     lax.fori_loop(0, slots, forward, 0, unroll=32)
 
-    def fill(c2):
-        for w in range(3):
-            s_buf[c2, w] = prod_f[links_s[1, 3 * c2 + w]].astype(BF16)
+    def fill(c2, w):
+        s_buf[c2, w] = prod_f[links_s[1, 3 * c2 + w]].astype(BF16)
+
+    sent = []
+
+    def send(src, dst, send_sem, recv_sem, device):
+        cp = remote(src, dst, send_sem, recv_sem, device)
+        cp.start()
+        sent.append(cp)
+        return cp
 
     offs = far_first(n_z) + [0]
-    p3a = []
-    for j, off in enumerate(offs):
-        c2 = 2 * ((z + off) % n_z) + 1 - h
-        fill(c2)
-        cp = remote(s_buf.at[c2], yh_recv.at[j], p3a_s.at[j], p3a_r.at[j], y_partner)
-        cp.start()
-        p3a.append(cp)
-    for j, off in enumerate(offs):
-        fill(2 * ((z + off) % n_z) + h)
-    p3b = []
-    for j, off in enumerate(offs):
-        c2 = 2 * ((z + off) % n_z) + h
-        p3a[j].wait_recv()
-        both = s_buf[c2].astype(F32) + yh_recv[j].astype(F32)
-        if off:
-            t_buf[j] = both.astype(BF16)
-            cp = remote(t_buf.at[j], z_recv.at[j], p3b_s.at[j], p3b_r.at[j], z_peer(off))
-            cp.start()
-            p3b.append(cp)
-        else:
-            hidden = both
-    for j in range(n_z - 1):
-        p3b[j].wait_recv()
-        hidden = hidden + z_recv[j].astype(F32)
-
+    p3a = [[], [], []]
+    for w in range(3):
+        for j, off in enumerate(offs):
+            c2 = 2 * ((z + off) % n_z) + 1 - h
+            fill(c2, w)
+            p3a[w].append(send(s_buf.at[c2, w], yh_recv.at[j, w], p3a_s.at[j, w], p3a_r.at[j, w], y_partner))
+    for w in range(3):
+        for off in offs:
+            fill(2 * ((z + off) % n_z) + h, w)
+    p3b = [[], [], []]
+    own_part = [None] * 3
+
+    def sum_h(w):
+        for j, off in enumerate(offs):
+            c2 = 2 * ((z + off) % n_z) + h
+            p3a[w][j].wait_recv()
+            both = s_buf[c2, w].astype(F32) + yh_recv[j, w].astype(F32)
+            if off:
+                t_buf[j, w] = both.astype(BF16)
+                p3b[w].append(send(t_buf.at[j, w], z_recv.at[j, w], p3b_s.at[j, w], p3b_r.at[j, w], z_peer(off)))
+            else:
+                own_part[w] = both
+
+    def place(dist, w):
+        return hg_buf.at[3 * (2 * ((z + 2 * n_z - dist) % n_z) + h) + w]
+
+    def z_send(what, j, off, w):
+        send(what, what, p4z_s.at[j, w], p4z_r.at[j, w], z_peer(off))
+
+    def y_send_on(what, j, w):
+        send(what, what, p4y_s.at[j, w], p4y_r.at[j, w], y_partner)
+
+    def arrived(j, dist, w):
+        got = place(dist, w)
+        remote(got, got, p4z_s.at[j, w], p4z_r.at[j, w], y_partner).wait_recv()
+        return got
+
+    def activate(w):
+        hidden = own_part[w]
+        for j in range(n_z - 1):
+            p3b[w][j].wait_recv()
+            hidden = hidden + z_recv[j, w].astype(F32)
+        sigma = jax.nn.sigmoid(hidden)
+        grad = cot_v[w].astype(F32) * (sigma * (1.0 + hidden * (1.0 - sigma)))
+        hg_buf[3 * c + w] = grad.astype(BF16)
+        act_v[w] = (hidden * sigma).astype(BF16)
+        own = hg_buf.at[3 * c + w]
+        if w == 2:
+            z_send(own, 6, 4, w)
+            z_send(own, 4, 3, w)
+            z_send(own, 5, n_z - 3, w)
+        z_send(own, 2, 2, w)
+        z_send(own, 3, n_z - 2, w)
+        z_send(own, 0, 1, w)
+        z_send(own, 1, n_z - 1, w)
+        y_send_on(own, n_z - 1, w)
+
+    side = 1 - 2 * (z % 2)
+
+    def pass_on(w):
+        if w < 2:
+            plus = arrived(2, 2, w)
+            z_send(plus, 4, 1, w)
+            minus = arrived(3, n_z - 2, w)
+            z_send(minus, 5, n_z - 1, w)
+            z_send(place(2 * side + n_z, w), 6, 2 * side + n_z, w)
+        y_send_on(arrived(0, 1, w), 0, w)
+        y_send_on(arrived(1, n_z - 1, w), 1, w)
+        if w == 2:
+            plus = arrived(2, 2, w)
+            minus = arrived(3, n_z - 2, w)
+        y_send_on(plus, 2, w)
+        y_send_on(minus, 3, w)
+
+    def last_on(w):
+        y_send_on(arrived(4, 3, w), 4, w)
+        y_send_on(arrived(5, n_z - 3, w), 5, w)
+        y_send_on(arrived(6, 4, w), 6, w)
+
+    sum_h(0)
+    sum_h(1)
+    sum_h(2)
     in_c.wait()
-    sigma = jax.nn.sigmoid(hidden)
-    grad = cot_v[...].astype(F32) * (sigma * (1.0 + hidden * (1.0 - sigma)))
-    hg_buf[pl.ds(3 * c, 3)] = grad.astype(BF16)
-    act_v[...] = (hidden * sigma).astype(BF16)
-
-    own = hg_buf.at[pl.ds(3 * c, 3)]
-    p4y = [remote(own, own, p4y_s.at[n_z - 1], p4y_r.at[n_z - 1], y_partner)]
-    p4y[0].start()
-    def z_got(dist):
-        return hg_buf.at[pl.ds(3 * (2 * ((z + 2 * n_z - dist) % n_z) + h), 3)]
-
-    p4z = []
-
-    def z_send(what, j, off):
-        cp = remote(what, what, p4z_s.at[j], p4z_r.at[j], z_peer(off))
-        cp.start()
-        p4z.append(cp)
-
-    def arrived(j, dist):
-        got = z_got(dist)
-        remote(got, got, p4z_s.at[j], p4z_r.at[j], y_partner).wait_recv()
-        return got
-
-    def y_forward(got, j):
-        cp = remote(got, got, p4y_s.at[j], p4y_r.at[j], y_partner)
-        cp.start()
-        p4y.append(cp)
-
-    side = 1 - 2 * (z % 2)
-    z_send(own, 2, 2)
-    z_send(own, 3, n_z - 2)
-    z_send(own, 0, 1)
-    z_send(own, 1, n_z - 1)
-    y_forward(arrived(0, 1), 0)
-    y_forward(arrived(1, n_z - 1), 1)
-    plus = arrived(2, 2)
-    z_send(plus, 4, 1)
-    minus = arrived(3, n_z - 2)
-    z_send(minus, 5, n_z - 1)
-    z_send(hg_buf.at[pl.ds(3 * (2 * ((z + n_z - 2 * side) % n_z) + h), 3)], 6, 2 * side + n_z)
-    y_forward(plus, 2)
-    y_forward(minus, 3)
+    activate(0)
+    activate(1)
+    pass_on(0)
+    activate(2)
     act_cols = pl.ds(pl.multiple_of(b * 128, 128), 128)
     act_dst = act_out.at[:, a, :, act_cols]
     local = pltpu.make_async_copy(act_v, act_dst, in_sem.at[3])
     local.start()
+    pass_on(1)
+    last_on(0)
+    pass_on(2)
     acts = []
     for k in range(1, 4):
         cp = remote(act_v, act_dst, act_s.at[k - 1], act_r.at[k - 1], feat_peers[k - 1])
         cp.start()
         acts.append(cp)
-    y_forward(arrived(4, 3), 4)
-    y_forward(arrived(5, n_z - 3), 5)
-    y_forward(arrived(6, 4), 6)
-    for j, dist in enumerate([1, n_z - 1, 2, n_z - 2, 3, n_z - 3, 4, 0]):
-        got = hg_buf.at[pl.ds(3 * (2 * ((z + n_z - dist) % n_z) + 1 - h), 3)]
-        remote(got, got, p4y_s.at[j], p4y_r.at[j], y_partner).wait_recv()
+    last_on(1)
+    last_on(2)
+    for w in range(3):
+        for j, dist in enumerate([1, n_z - 1, 2, n_z - 2, 3, n_z - 3, 4, 0]):
+            got = hg_buf.at[3 * (2 * ((z + n_z - dist) % n_z) + 1 - h) + w]
+            remote(got, got, p4y_s.at[j, w], p4y_r.at[j, w], y_partner).wait_recv()
 
     def backward(s, _):
         prod_b[s] = lax.dot_general(
@@ -356,7 +389,7 @@
         remote(act_v, got, act_s.at[k - 1], act_r.at[k - 1], y_partner).wait_recv()
     local.wait()
     local_wg.wait()
-    for cp in copies + p2 + p3a + p3b + p4y + p4z + acts + p5 + p6 + k1 + k2 + k3 + [xg, bc]:
+    for cp in copies + p2 + sent + acts + p5 + p6 + k1 + k2 + k3 + [xg, bc]:
         cp.wait_send()
 
 
@@ -372,7 +405,8 @@
     smem = pl.BlockSpec(memory_space=pltpu.SMEM)
     vmem = pl.BlockSpec(memory_space=pltpu.VMEM)
     hbm = pl.BlockSpec(memory_space=pltpu.HBM)
-    sem_counts = [12, 3, 3, n_g - 1, n_g - 1, n_z, n_z, n_z - 1, n_z - 1, 3, 3, n_z - 1, n_z - 1, n_z, n_z,
+    sem_counts = [12, (3, 3), (3, 3), (n_g - 1, 3), (n_g - 1, 3), (n_z, 3), (n_z, 3), (n_z - 1, 3), (n_z - 1, 3),
+                  3, 3, (n_z - 1, 3), (n_z - 1, 3), (n_z, 3), (n_z, 3),
                   1, 1, 1, 1, n_g - 1, n_g - 1, 3, 3, 2 * n_g - 1, 2 * n_g - 1, n_z - 1, n_z - 1, n_g - 1, n_g - 1]
     act, fg, wg = pl.pallas_call(
         functools.partial(kernel, n_row, n_z, slots, node_dev * n_row * n_col),
@@ -412,7 +446,7 @@
             pltpu.VMEM((2 * n_g - 1, piece_rows, 128), BF16),
             pltpu.VMEM((n_z, piece_rows, 128), BF16),
             pltpu.VMEM((piece_rows, 128), F32),
-        ] + [dma((n,)) for n in sem_counts],
+        ] + [dma(n if isinstance(n, tuple) else (n,)) for n in sem_counts],
         compiler_params=pltpu.CompilerParams(
             collective_id=0, has_side_effects=True, vmem_limit_bytes=40 * 1024 * 1024),
     )(

time: 74.4 us -> 72 us (0.968)
  Pallas kernels: 71 us -> 68.6 us
    pallas_call x1, Pallas kernels: 71 us -> 68.6 us  [shards(): pl.pallas_call(functools.partial(kernel, n_row, n_z, slots, node_dev * n_...]
where the time goes in v6:
time: 72 us; the launch traced here: 71.9 us
  Pallas kernels  68.6 us (95%)
  local copies, waits for them, and re-layouts  2.02 us (3%)
  between operations  1.29 us (2%)
    pallas_call x1, Pallas kernels, shards(): pl.pallas_call(functools.partial(kernel, n_row, n_z, slots, node_dev * n_...  68.6 us
    unnamed x3, local copies, waits for them, and re-layouts  2.02 us

profile of v6, /device:TPU:1, one launch (start us, length us, event | category | flops | bytes accessed | tf_op | source)
XLA Modules:
  0.0 71.9 jit_solution(14765384659901297238)
XLA Ops:
  1.3 68.6 %shard_map.94 = (bf16[3,2,64,256]{3,2,1,0:T(8,128)(2,1)S(1)}, bf16[192,384]{1,0:T(8,128)(2,1)S(1)}, f32[192,256]{1,0:T(8,128)S(1)}) custom-call(s32[1,64]{1,0:T(1,128)} %bitcast.14, s32[1,64]{1,0:T(1,128)} %bitcast.15, s32[1,1]{1,0:T(1,128)S(6)} %copy.13.count_s, bf16[192,1536]{1,0:T(8,128)(2,1)} %bitcast.12, bf16[192,256]{1,0:T(8,128)(2,1)} %w_hbm.1, ...), custom_call_target="tpu_custom_call" | custom-call | tf_op jit(solution)/shard_map/pallas_call | solution.py:411
  69.9 0.7 copy.14
  70.6 0.7 copy.15
  71.2 0.7 copy.16

commit v7 on v6

--- a/solution.py
+++ b/solution.py
@@ -27,7 +27,7 @@
     s_buf, yh_recv, t_buf, z_recv, hg_buf, act_v,
     prod_b, b_both, b_recv, b_full,
     xt_both, u_send, u_recv, v_buf, wg_piece,
-    in_sem, p1_s, p1_r, p2_s, p2_r, p3a_s, p3a_r, p3b_s, p3b_r,
+    here_sem, in_sem, p1_s, p1_r, p2_s, p2_r, p3a_s, p3a_r, p3b_s, p3b_r,
     act_s, act_r, p4z_s, p4z_r, p4y_s, p4y_r, xg_s, xg_r, bc_s, bc_r, p5_s, p5_r, p6_s, p6_r,
     k1_s, k1_r, k2_s, k2_r, k3_s, k3_r,
 ):
@@ -83,10 +83,8 @@
     for k in range(1, n_row):
         peers.append({"row": (r + k) % n_row})
         peers.append({"feat": (f + 2) % 4, "row": (r + k) % n_row})
-    peers += [z_peer(k) for k in range(1, n_z)]
+    peers += [z_peer(k) for k in (1, n_z - 1)]
     peers.append(y_partner)
-    peers += [{"row": (r + k) % n_row, "col": c + 1 - 2 * h} for k in range(n_row)]
-    peers += [{"feat": (f + 2) % 4, "row": (r + k) % n_row, "col": c + 1 - 2 * h} for k in range(1, n_row)]
     for peer in reversed(peers):
         pl.semaphore_signal(barrier, inc=1, device_id=peer, device_id_type=MESH)
     for cp in in_keys:
@@ -104,6 +102,8 @@
         for core in range(2):
             y_send[2 * q + core] = y_part[192 * q:192 * (q + 1), 128 * core:128 * (core + 1)].reshape(3, 64, 128)
     pl.semaphore_wait(barrier, len(peers))
+    for k in (1, n_z - 1):
+        pl.semaphore_signal(here_sem.at[0], inc=1, device_id=z_peer(k), device_id_type=MESH)
 
     copies = []
     p1 = [[], [], []]
@@ -132,6 +132,10 @@
             links_v[pl.ds(2 * i + w, 1), :] = jnp.where(top < 0, slots, top)
     links = pltpu.make_async_copy(links_v, links_s, in_sem.at[10])
     links.start()
+    pl.semaphore_wait(here_sem.at[0], 2)
+    for k in (2, n_z - 2):
+        pl.semaphore_signal(here_sem.at[1], inc=1, device_id=z_peer(k), device_id_type=MESH)
+
     g = 2 * r + a
     p2 = []
     for w in range(3):
@@ -154,6 +158,8 @@
         for k in range(1, n_g):
             got = y_buf.at[3 * ((g + n_g - k) % n_g) + w]
             remote(got, got, p2_s.at[k - 1, w], p2_r.at[k - 1, w], y_partner).wait_recv()
+
+    pl.semaphore_wait(here_sem.at[1], 2)
 
     xg = remote(feat_hbm, xt_both.at[y_low], xg_s.at[0], xg_r.at[0], {"feat": (f + 2) % 4})
     xg.start()
@@ -256,11 +262,11 @@
         y_send_on(arrived(5, n_z - 3, w), 5, w)
         y_send_on(arrived(6, 4, w), 6, w)
 
+    in_c.wait()
     sum_h(0)
     sum_h(1)
+    activate(0)
     sum_h(2)
-    in_c.wait()
-    activate(0)
     activate(1)
     pass_on(0)
     activate(2)
@@ -446,6 +452,7 @@
             pltpu.VMEM((2 * n_g - 1, piece_rows, 128), BF16),
             pltpu.VMEM((n_z, piece_rows, 128), BF16),
             pltpu.VMEM((piece_rows, 128), F32),
+            pltpu.SemaphoreType.REGULAR((2,)),
         ] + [dma(n if isinstance(n, tuple) else (n,)) for n in sem_counts],
         compiler_params=pltpu.CompilerParams(
             collective_id=0, has_side_effects=True, vmem_limit_bytes=40 * 1024 * 1024),

time: 72 us -> 71 us (0.986)
  Pallas kernels: 68.6 us -> 67.6 us
    pallas_call x1, Pallas kernels: 68.6 us -> 67.6 us  [shards(): pl.pallas_call(functools.partial(kernel, n_row, n_z, slots, node_dev * n_...]
where the time goes in v7:
time: 71 us; the launch traced here: 70.9 us
  Pallas kernels  67.6 us (95%)
  local copies, waits for them, and re-layouts  2.02 us (3%)
  between operations  1.29 us (2%)
    pallas_call x1, Pallas kernels, shards(): pl.pallas_call(functools.partial(kernel, n_row, n_z, slots, node_dev * n_...  67.6 us
    unnamed x3, local copies, waits for them, and re-layouts  2.02 us

profile of v7, /device:TPU:1, one launch (start us, length us, event | category | flops | bytes accessed | tf_op | source)
XLA Modules:
  0.0 70.9 jit_solution(12370152120586919417)
XLA Ops:
  1.3 67.6 %shard_map.94 = (bf16[3,2,64,256]{3,2,1,0:T(8,128)(2,1)S(1)}, bf16[192,384]{1,0:T(8,128)(2,1)S(1)}, f32[192,256]{1,0:T(8,128)S(1)}) custom-call(s32[1,64]{1,0:T(1,128)} %bitcast.14, s32[1,64]{1,0:T(1,128)} %bitcast.15, s32[1,1]{1,0:T(1,128)S(6)} %copy.13.count_s, bf16[192,1536]{1,0:T(8,128)(2,1)} %bitcast.12, bf16[192,256]{1,0:T(8,128)(2,1)} %w_hbm.1, ...), custom_call_target="tpu_custom_call" | custom-call | tf_op jit(solution)/shard_map/pallas_call | solution.py:417
  68.9 0.7 copy.14
  69.6 0.7 copy.15
  70.2 0.7 copy.16

commit v8 on v7

--- a/solution.py
+++ b/solution.py
@@ -80,7 +80,8 @@
 
     barrier = pltpu.get_barrier_semaphore()
     peers = list(feat_peers)
-    for k in range(1, n_row):
+    x_sides = (1, n_row - 1) if n_row > 1 else ()
+    for k in x_sides:
         peers.append({"row": (r + k) % n_row})
         peers.append({"feat": (f + 2) % 4, "row": (r + k) % n_row})
     peers += [z_peer(k) for k in (1, n_z - 1)]
@@ -104,6 +105,8 @@
     pl.semaphore_wait(barrier, len(peers))
     for k in (1, n_z - 1):
         pl.semaphore_signal(here_sem.at[0], inc=1, device_id=z_peer(k), device_id_type=MESH)
+    for k in x_sides:
+        pl.semaphore_signal(here_sem.at[2], inc=1, device_id={"row": (r + k) % n_row}, device_id_type=MESH)
 
     copies = []
     p1 = [[], [], []]
@@ -133,6 +136,8 @@
     links = pltpu.make_async_copy(links_v, links_s, in_sem.at[10])
     links.start()
     pl.semaphore_wait(here_sem.at[0], 2)
+    if x_sides:
+        pl.semaphore_wait(here_sem.at[2], 2)
     for k in (2, n_z - 2):
         pl.semaphore_signal(here_sem.at[1], inc=1, device_id=z_peer(k), device_id_type=MESH)
 
@@ -277,13 +282,13 @@
     pass_on(1)
     last_on(0)
     pass_on(2)
+    last_on(1)
+    last_on(2)
     acts = []
     for k in range(1, 4):
         cp = remote(act_v, act_dst, act_s.at[k - 1], act_r.at[k - 1], feat_peers[k - 1])
         cp.start()
         acts.append(cp)
-    last_on(1)
-    last_on(2)
     for w in range(3):
         for j, dist in enumerate([1, n_z - 1, 2, n_z - 2, 3, n_z - 3, 4, 0]):
             got = hg_buf.at[3 * (2 * ((z + n_z - dist) % n_z) + 1 - h) + w]
@@ -452,7 +457,7 @@
             pltpu.VMEM((2 * n_g - 1, piece_rows, 128), BF16),
             pltpu.VMEM((n_z, piece_rows, 128), BF16),
             pltpu.VMEM((piece_rows, 128), F32),
-            pltpu.SemaphoreType.REGULAR((2,)),
+            pltpu.SemaphoreType.REGULAR((3,)),
         ] + [dma(n if isinstance(n, tuple) else (n,)) for n in sem_counts],
         compiler_params=pltpu.CompilerParams(
             collective_id=0, has_side_effects=True, vmem_limit_bytes=40 * 1024 * 1024),

time: 71 us -> 70.8 us (level)
  no operation moved by 1% of the time
where the time goes in v8:
time: 70.8 us; the launch traced here: 70.7 us
  Pallas kernels  67.4 us (95%)
  local copies, waits for them, and re-layouts  2.02 us (3%)
  between operations  1.29 us (2%)
    pallas_call x1, Pallas kernels, shards(): pl.pallas_call(functools.partial(kernel, n_row, n_z, slots, node_dev * n_...  67.4 us
    unnamed x3, local copies, waits for them, and re-layouts  2.02 us

profile of v8, /device:TPU:1, one launch (start us, length us, event | category | flops | bytes accessed | tf_op | source)
XLA Modules:
  0.0 70.7 jit_solution(16973094559022411035)
XLA Ops:
  1.3 67.4 %shard_map.94 = (bf16[3,2,64,256]{3,2,1,0:T(8,128)(2,1)S(1)}, bf16[192,384]{1,0:T(8,128)(2,1)S(1)}, f32[192,256]{1,0:T(8,128)S(1)}) custom-call(s32[1,64]{1,0:T(1,128)} %bitcast.14, s32[1,64]{1,0:T(1,128)} %bitcast.15, s32[1,1]{1,0:T(1,128)S(6)} %copy.13.count_s, bf16[192,1536]{1,0:T(8,128)(2,1)} %bitcast.12, bf16[192,256]{1,0:T(8,128)(2,1)} %w_hbm.1, ...), custom_call_target="tpu_custom_call" | custom-call | tf_op jit(solution)/shard_map/pallas_call | solution.py:422
  68.7 0.7 copy.14
  69.4 0.7 copy.15
  70.0 0.7 copy.16

commit v9 on v8

--- a/solution.py
+++ b/solution.py
@@ -143,6 +143,7 @@
 
     g = 2 * r + a
     p2 = []
+    g_order = sorted(range(1, n_g), key=lambda k: -min(k, n_g - k))
     for w in range(3):
         total = y_send[2 * a + b, w].astype(F32)
         for k in range(3):
@@ -150,19 +151,17 @@
             total = total + y_recv[k, w].astype(F32)
         y_buf[3 * g + w] = total.astype(BF16)
         mine = y_buf.at[3 * g + w]
-        for k in range(1, n_g):
+        for k in g_order:
             _, dev = g_peer(k)
-            cp = remote(mine, mine, p2_s.at[k - 1, w], p2_r.at[k - 1, w], dev)
+            cp = remote(mine, mine, p2_s.at[k - 1, w], p2_r.at[0], dev)
             cp.start()
             p2.append(cp)
     prod_f[slots] = jnp.zeros((64, 128), F32)
     prod_b[slots] = jnp.zeros((128, 128), F32)
     in_t.wait()
     links.wait()
-    for w in range(3):
-        for k in range(1, n_g):
-            got = y_buf.at[3 * ((g + n_g - k) % n_g) + w]
-            remote(got, got, p2_s.at[k - 1, w], p2_r.at[k - 1, w], y_partner).wait_recv()
+    got = y_buf.at[pl.ds(0, 3 * (n_g - 1))]
+    remote(got, got, p2_s.at[0, 0], p2_r.at[0], y_partner).wait_recv()
 
     pl.semaphore_wait(here_sem.at[1], 2)
 
@@ -218,7 +217,7 @@
         send(what, what, p4z_s.at[j, w], p4z_r.at[j, w], z_peer(off))
 
     def y_send_on(what, j, w):
-        send(what, what, p4y_s.at[j, w], p4y_r.at[j, w], y_partner)
+        send(what, what, p4y_s.at[j, w], p4y_r.at[0], y_partner)
 
     def arrived(j, dist, w):
         got = place(dist, w)
@@ -289,10 +288,8 @@
         cp = remote(act_v, act_dst, act_s.at[k - 1], act_r.at[k - 1], feat_peers[k - 1])
         cp.start()
         acts.append(cp)
-    for w in range(3):
-        for j, dist in enumerate([1, n_z - 1, 2, n_z - 2, 3, n_z - 3, 4, 0]):
-            got = hg_buf.at[3 * (2 * ((z + n_z - dist) % n_z) + 1 - h) + w]
-            remote(got, got, p4y_s.at[j, w], p4y_r.at[j, w], y_partner).wait_recv()
+    got = hg_buf.at[pl.ds(0, 3 * n_z)]
+    remote(got, got, p4y_s.at[0, 0], p4y_r.at[0], y_partner).wait_recv()
 
     def backward(s, _):
         prod_b[s] = lax.dot_general(
@@ -345,6 +342,8 @@
         cp = remote(v_buf.at[z], v_buf.at[z], k2_s.at[j], k2_r.at[j], z_peer(off))
         cp.start()
         k2.append(cp)
+    for cp in copies + p2 + sent + acts + p5 + k1 + [xg, bc]:
+        cp.wait_send()
 
     total = b_both[b, pl.ds(3 * g, 3)].astype(F32)
     for k in range(n_g - 1):
@@ -400,7 +399,7 @@
         remote(act_v, got, act_s.at[k - 1], act_r.at[k - 1], y_partner).wait_recv()
     local.wait()
     local_wg.wait()
-    for cp in copies + p2 + sent + acts + p5 + p6 + k1 + k2 + k3 + [xg, bc]:
+    for cp in p6 + k2 + k3:
         cp.wait_send()
 
 
@@ -416,8 +415,8 @@
     smem = pl.BlockSpec(memory_space=pltpu.SMEM)
     vmem = pl.BlockSpec(memory_space=pltpu.VMEM)
     hbm = pl.BlockSpec(memory_space=pltpu.HBM)
-    sem_counts = [12, (3, 3), (3, 3), (n_g - 1, 3), (n_g - 1, 3), (n_z, 3), (n_z, 3), (n_z - 1, 3), (n_z - 1, 3),
-                  3, 3, (n_z - 1, 3), (n_z - 1, 3), (n_z, 3), (n_z, 3),
+    sem_counts = [12, (3, 3), (3, 3), (n_g - 1, 3), 1, (n_z, 3), (n_z, 3), (n_z - 1, 3), (n_z - 1, 3),
+                  3, 3, (n_z - 1, 3), (n_z - 1, 3), (n_z, 3), 1,
                   1, 1, 1, 1, n_g - 1, n_g - 1, 3, 3, 2 * n_g - 1, 2 * n_g - 1, n_z - 1, n_z - 1, n_g - 1, n_g - 1]
     act, fg, wg = pl.pallas_call(
         functools.partial(kernel, n_row, n_z, slots, node_dev * n_row * n_col),

time: 70.8 us -> 69.6 us (0.983)
  Pallas kernels: 67.4 us -> 66.2 us
    pallas_call x1, Pallas kernels: 67.4 us -> 66.2 us  [shards(): pl.pallas_call(functools.partial(kernel, n_row, n_z, slots, node_dev * n_...]
where the time goes in v9:
time: 69.6 us; the launch traced here: 69.5 us
  Pallas kernels  66.2 us (95%)
  local copies, waits for them, and re-layouts  2.02 us (3%)
  between operations  1.29 us (2%)
    pallas_call x1, Pallas kernels, shards(): pl.pallas_call(functools.partial(kernel, n_row, n_z, slots, node_dev * n_...  66.2 us
    unnamed x3, local copies, waits for them, and re-layouts  2.02 us

profile of v9, /device:TPU:1, one launch (start us, length us, event | category | flops | bytes accessed | tf_op | source)
XLA Modules:
  0.0 69.5 jit_solution(4661991312289572036)
XLA Ops:
  1.3 66.2 %shard_map.94 = (bf16[3,2,64,256]{3,2,1,0:T(8,128)(2,1)S(1)}, bf16[192,384]{1,0:T(8,128)(2,1)S(1)}, f32[192,256]{1,0:T(8,128)S(1)}) custom-call(s32[1,64]{1,0:T(1,128)} %bitcast.14, s32[1,64]{1,0:T(1,128)} %bitcast.15, s32[1,1]{1,0:T(1,128)S(6)} %copy.13.count_s, bf16[192,1536]{1,0:T(8,128)(2,1)} %bitcast.12, bf16[192,256]{1,0:T(8,128)(2,1)} %w_hbm.1, ...), custom_call_target="tpu_custom_call" | custom-call | tf_op jit(solution)/shard_map/pallas_call | solution.py:421
  67.5 0.7 copy.14
  68.1 0.7 copy.15
  68.8 0.7 copy.16

commit v10 on v9

--- a/solution.py
+++ b/solution.py
@@ -206,7 +206,7 @@
             both = s_buf[c2, w].astype(F32) + yh_recv[j, w].astype(F32)
             if off:
                 t_buf[j, w] = both.astype(BF16)
-                p3b[w].append(send(t_buf.at[j, w], z_recv.at[j, w], p3b_s.at[j, w], p3b_r.at[j, w], z_peer(off)))
+                p3b[w].append(send(t_buf.at[j, w], z_recv.at[j, w], p3b_s.at[j, w], p3b_r.at[w], z_peer(off)))
             else:
                 own_part[w] = both
 
@@ -226,8 +226,9 @@
 
     def activate(w):
         hidden = own_part[w]
+        got = z_recv.at[pl.ds(0, n_z - 1), w]
+        remote(got, got, p3b_s.at[0, w], p3b_r.at[w], y_partner).wait_recv()
         for j in range(n_z - 1):
-            p3b[w][j].wait_recv()
             hidden = hidden + z_recv[j, w].astype(F32)
         sigma = jax.nn.sigmoid(hidden)
         grad = cot_v[w].astype(F32) * (sigma * (1.0 + hidden * (1.0 - sigma)))
@@ -321,33 +322,33 @@
         q2 = (n_g * y_low + u + k) % (2 * n_g)
         low2, u2 = q2 // n_g, q2 % n_g
         dev = {"feat": 2 * low2 + b, "row": u2 // 2, "col": 2 * z + u2 % 2}
-        cp = remote(u_send.at[low2, u2], u_recv.at[k - 1], k1_s.at[k - 1], k1_r.at[k - 1], dev)
+        cp = remote(u_send.at[low2, u2], u_recv.at[k - 1], k1_s.at[k - 1], k1_r.at[0], dev)
         cp.start()
         k1.append(cp)
 
     p5 = []
     for k in range(1, n_g):
         g2, dev = g_peer(k)
-        cp = remote(b_both.at[b, pl.ds(3 * g2, 3)], b_recv.at[k - 1], p5_s.at[k - 1], p5_r.at[k - 1], dev)
+        cp = remote(b_both.at[b, pl.ds(3 * g2, 3)], b_recv.at[k - 1], p5_s.at[k - 1], p5_r.at[0], dev)
         cp.start()
         p5.append(cp)
 
     total = u_send[y_low, u].astype(F32)
+    remote(u_recv, u_recv, k1_s.at[0], k1_r.at[0], y_partner).wait_recv()
     for k in range(2 * n_g - 1):
-        k1[k].wait_recv()
         total = total + u_recv[k].astype(F32)
     v_buf[z] = total.astype(BF16)
     k2 = []
     for j, off in enumerate(offs[:-1]):
-        cp = remote(v_buf.at[z], v_buf.at[z], k2_s.at[j], k2_r.at[j], z_peer(off))
+        cp = remote(v_buf.at[z], v_buf.at[z], k2_s.at[j], k2_r.at[0], z_peer(off))
         cp.start()
         k2.append(cp)
     for cp in copies + p2 + sent + acts + p5 + k1 + [xg, bc]:
         cp.wait_send()
 
     total = b_both[b, pl.ds(3 * g, 3)].astype(F32)
+    remote(b_recv, b_recv, p5_s.at[0], p5_r.at[0], y_partner).wait_recv()
     for k in range(n_g - 1):
-        p5[k].wait_recv()
         total = total + b_recv[k].astype(F32)
     b_full[2 * b + a] = total.astype(BF16)
     mine = b_full.at[2 * b + a]
@@ -357,9 +358,8 @@
         cp.start()
         p6.append(cp)
 
-    for j, off in enumerate(offs[:-1]):
-        got = v_buf.at[(z + n_z - off) % n_z]
-        remote(got, got, k2_s.at[j], k2_r.at[j], y_partner).wait_recv()
+    got = v_buf.at[pl.ds(0, n_z - 1)]
+    remote(got, got, k2_s.at[0], k2_r.at[0], y_partner).wait_recv()
     total = v_buf[0].astype(F32)
     for j in range(1, n_z):
         total = total + v_buf[j].astype(F32)
@@ -415,9 +415,9 @@
     smem = pl.BlockSpec(memory_space=pltpu.SMEM)
     vmem = pl.BlockSpec(memory_space=pltpu.VMEM)
     hbm = pl.BlockSpec(memory_space=pltpu.HBM)
-    sem_counts = [12, (3, 3), (3, 3), (n_g - 1, 3), 1, (n_z, 3), (n_z, 3), (n_z - 1, 3), (n_z - 1, 3),
+    sem_counts = [12, (3, 3), (3, 3), (n_g - 1, 3), 1, (n_z, 3), (n_z, 3), (n_z - 1, 3), 3,
                   3, 3, (n_z - 1, 3), (n_z - 1, 3), (n_z, 3), 1,
-                  1, 1, 1, 1, n_g - 1, n_g - 1, 3, 3, 2 * n_g - 1, 2 * n_g - 1, n_z - 1, n_z - 1, n_g - 1, n_g - 1]
+                  1, 1, 1, 1, n_g - 1, 1, 3, 3, 2 * n_g - 1, 1, n_z - 1, 1, n_g - 1, n_g - 1]
     act, fg, wg = pl.pallas_call(
         functools.partial(kernel, n_row, n_z, slots, node_dev * n_row * n_col),
         out_shape=[

time: 69.6 us -> 69.2 us (level)
  no operation moved by 1% of the time
where the time goes in v10:
time: 69.2 us; the launch traced here: 69.1 us
  Pallas kernels  65.8 us (95%)
  local copies, waits for them, and re-layouts  2.02 us (3%)
  between operations  1.29 us (2%)
    pallas_call x1, Pallas kernels, shards(): pl.pallas_call(functools.partial(kernel, n_row, n_z, slots, node_dev * n_...  65.8 us
    unnamed x3, local copies, waits for them, and re-layouts  2.02 us

profile of v10, /device:TPU:1, one launch (start us, length us, event | category | flops | bytes accessed | tf_op | source)
XLA Modules:
  0.0 69.1 jit_solution(16270138298991379744)
XLA Ops:
  1.3 65.8 %shard_map.94 = (bf16[3,2,64,256]{3,2,1,0:T(8,128)(2,1)S(1)}, bf16[192,384]{1,0:T(8,128)(2,1)S(1)}, f32[192,256]{1,0:T(8,128)S(1)}) custom-call(s32[1,64]{1,0:T(1,128)} %bitcast.14, s32[1,64]{1,0:T(1,128)} %bitcast.15, s32[1,1]{1,0:T(1,128)S(6)} %copy.13.count_s, bf16[192,1536]{1,0:T(8,128)(2,1)} %bitcast.12, bf16[192,256]{1,0:T(8,128)(2,1)} %w_hbm.1, ...), custom_call_target="tpu_custom_call" | custom-call | tf_op jit(solution)/shard_map/pallas_call | solution.py:421
  67.1 0.7 copy.14
  67.8 0.7 copy.15
  68.4 0.7 copy.16

commit v11 on v10

--- a/solution.py
+++ b/solution.py
@@ -109,15 +109,13 @@
         pl.semaphore_signal(here_sem.at[2], inc=1, device_id={"row": (r + k) % n_row}, device_id_type=MESH)
 
     copies = []
-    p1 = [[], [], []]
     for w in range(3):
         for k in range(1, 4):
             f2 = (f + k) % 4
             piece = ((f2 // 2 + h) % 2) * 2 + f2 % 2
-            cp = remote(y_send.at[piece, w], y_recv.at[k - 1, w], p1_s.at[k - 1, w], p1_r.at[k - 1, w], feat_peers[k - 1])
+            cp = remote(y_send.at[piece, w], y_recv.at[k - 1, w], p1_s.at[k - 1, w], p1_r.at[w], feat_peers[k - 1])
             cp.start()
             copies.append(cp)
-            p1[w].append(cp)
     for cp in in_keys:
         cp.wait()
     ids = lax.broadcasted_iota(jnp.int32, (slots, 128), 0)
@@ -146,8 +144,9 @@
     g_order = sorted(range(1, n_g), key=lambda k: -min(k, n_g - k))
     for w in range(3):
         total = y_send[2 * a + b, w].astype(F32)
+        got = y_recv.at[:, w]
+        remote(got, got, p1_s.at[0, w], p1_r.at[w], y_partner).wait_recv()
         for k in range(3):
-            p1[w][k].wait_recv()
             total = total + y_recv[k, w].astype(F32)
         y_buf[3 * g + w] = total.astype(BF16)
         mine = y_buf.at[3 * g + w]
@@ -376,7 +375,7 @@
     k3 = []
     for k in range(1, n_g):
         _, dev = u_peer(k)
-        cp = remote(wg_piece, wg_place(u), k3_s.at[k - 1], k3_r.at[k - 1], dev)
+        cp = remote(wg_piece, wg_place(u), k3_s.at[k - 1], k3_r.at[0], dev)
         cp.start()
         k3.append(cp)
     for k in range(1, 4):
@@ -390,9 +389,6 @@
             (((1,), (1,)), ((), ())), preferred_element_type=F32)
     fg_out[...] = grad_t.astype(BF16)
 
-    for k in range(1, n_g):
-        got = wg_place((u + n_g - k) % n_g)
-        remote(wg_piece, got, k3_s.at[k - 1], k3_r.at[k - 1], y_partner).wait_recv()
     for k in range(1, 4):
         f2 = (f + 4 - k) % 4
         got = act_out.at[:, (f2 // 2 + h) % 2, :, pl.ds(pl.multiple_of((f2 % 2) * 128, 128), 128)]
@@ -401,6 +397,8 @@
     local_wg.wait()
     for cp in p6 + k2 + k3:
         cp.wait_send()
+    got = wg_out.at[pl.ds(0, wg_out.shape[0] // n_g * (n_g - 1))]
+    remote(got, got, k3_s.at[0], k3_r.at[0], y_partner).wait_recv()
 
 
 def shards(n_row, n_z, features, weight, tile_values, tile_rows, tile_cols, tile_count, cotangent):
@@ -415,9 +413,9 @@
     smem = pl.BlockSpec(memory_space=pltpu.SMEM)
     vmem = pl.BlockSpec(memory_space=pltpu.VMEM)
     hbm = pl.BlockSpec(memory_space=pltpu.HBM)
-    sem_counts = [12, (3, 3), (3, 3), (n_g - 1, 3), 1, (n_z, 3), (n_z, 3), (n_z - 1, 3), 3,
+    sem_counts = [12, (3, 3), 3, (n_g - 1, 3), 1, (n_z, 3), (n_z, 3), (n_z - 1, 3), 3,
                   3, 3, (n_z - 1, 3), (n_z - 1, 3), (n_z, 3), 1,
-                  1, 1, 1, 1, n_g - 1, 1, 3, 3, 2 * n_g - 1, 1, n_z - 1, 1, n_g - 1, n_g - 1]
+                  1, 1, 1, 1, n_g - 1, 1, 3, 3, 2 * n_g - 1, 1, n_z - 1, 1, n_g - 1, 1]
     act, fg, wg = pl.pallas_call(
         functools.partial(kernel, n_row, n_z, slots, node_dev * n_row * n_col),
         out_shape=[

time: 69.2 us -> 69.5 us (level)
  no operation moved by 1% of the time
where the time goes in v11:
time: 69.5 us; the launch traced here: 69.4 us
  Pallas kernels  66 us (95%)
  local copies, waits for them, and re-layouts  2.02 us (3%)
  between operations  1.29 us (2%)
    pallas_call x1, Pallas kernels, shards(): pl.pallas_call(functools.partial(kernel, n_row, n_z, slots, node_dev * n_...  66 us
    unnamed x3, local copies, waits for them, and re-layouts  2.02 us

profile of v11, /device:TPU:1, one launch (start us, length us, event | category | flops | bytes accessed | tf_op | source)
XLA Modules:
  0.0 69.4 jit_solution(9855849713459589495)
XLA Ops:
  1.3 66.0 %shard_map.94 = (bf16[3,2,64,256]{3,2,1,0:T(8,128)(2,1)S(1)}, bf16[192,384]{1,0:T(8,128)(2,1)S(1)}, f32[192,256]{1,0:T(8,128)S(1)}) custom-call(s32[1,64]{1,0:T(1,128)} %bitcast.14, s32[1,64]{1,0:T(1,128)} %bitcast.15, s32[1,1]{1,0:T(1,128)S(6)} %copy.13.count_s, bf16[192,1536]{1,0:T(8,128)(2,1)} %bitcast.12, bf16[192,256]{1,0:T(8,128)(2,1)} %w_hbm.1, ...), custom_call_target="tpu_custom_call" | custom-call | tf_op jit(solution)/shard_map/pallas_call | solution.py:419
  67.3 0.7 copy.14
  68.0 0.7 copy.15
  68.7 0.7 copy.16

commit v12 on v10

--- a/solution.py
+++ b/solution.py
@@ -299,11 +299,14 @@
 
     lax.fori_loop(0, slots, backward, 0, unroll=32)
 
-    for j in range(3 * n_row):
-        b_both[b, pl.ds(2 * j, 2)] = prod_b[links_s[3, j]].astype(BF16).reshape(2, 64, 128)
-
-    bc = remote(b_both.at[b], b_both.at[b], bc_s.at[0], bc_r.at[0], {"feat": f + 1 - 2 * b})
-    bc.start()
+    bc = []
+    for i in range(2):
+        for j in range(3 * n_row * i // 2, 3 * n_row * (i + 1) // 2):
+            b_both[b, pl.ds(2 * j, 2)] = prod_b[links_s[3, j]].astype(BF16).reshape(2, 64, 128)
+        half = b_both.at[b, pl.ds(3 * n_row * i, 3 * n_row)]
+        cp = remote(half, half, bc_s.at[i], bc_r.at[0], {"feat": f + 1 - 2 * b})
+        cp.start()
+        bc.append(cp)
 
     piece_rows = u_send.shape[2]
     in_xt.wait()
@@ -343,7 +346,7 @@
         cp = remote(v_buf.at[z], v_buf.at[z], k2_s.at[j], k2_r.at[0], z_peer(off))
         cp.start()
         k2.append(cp)
-    for cp in copies + p2 + sent + acts + p5 + k1 + [xg, bc]:
+    for cp in copies + p2 + sent + acts + p5 + k1 + bc + [xg]:
         cp.wait_send()
 
     total = b_both[b, pl.ds(3 * g, 3)].astype(F32)
@@ -417,7 +420,7 @@
     hbm = pl.BlockSpec(memory_space=pltpu.HBM)
     sem_counts = [12, (3, 3), (3, 3), (n_g - 1, 3), 1, (n_z, 3), (n_z, 3), (n_z - 1, 3), 3,
                   3, 3, (n_z - 1, 3), (n_z - 1, 3), (n_z, 3), 1,
-                  1, 1, 1, 1, n_g - 1, 1, 3, 3, 2 * n_g - 1, 1, n_z - 1, 1, n_g - 1, n_g - 1]
+                  1, 1, 2, 1, n_g - 1, 1, 3, 3, 2 * n_g - 1, 1, n_z - 1, 1, n_g - 1, n_g - 1]
     act, fg, wg = pl.pallas_call(
         functools.partial(kernel, n_row, n_z, slots, node_dev * n_row * n_col),
         out_shape=[

time: 69.2 us -> 69.2 us (level)
  no operation moved by 1% of the time
where the time goes in v12:
time: 69.2 us; the launch traced here: 69.1 us
  Pallas kernels  65.8 us (95%)
  local copies, waits for them, and re-layouts  2.02 us (3%)
  between operations  1.29 us (2%)
    pallas_call x1, Pallas kernels, shards(): pl.pallas_call(functools.partial(kernel, n_row, n_z, slots, node_dev * n_...  65.8 us
    unnamed x3, local copies, waits for them, and re-layouts  2.02 us

profile of v12, /device:TPU:1, one launch (start us, length us, event | category | flops | bytes accessed | tf_op | source)
XLA Modules:
  0.0 69.1 jit_solution(5444370001293360296)
XLA Ops:
  1.3 65.8 %shard_map.94 = (bf16[3,2,64,256]{3,2,1,0:T(8,128)(2,1)S(1)}, bf16[192,384]{1,0:T(8,128)(2,1)S(1)}, f32[192,256]{1,0:T(8,128)S(1)}) custom-call(s32[1,64]{1,0:T(1,128)} %bitcast.14, s32[1,64]{1,0:T(1,128)} %bitcast.15, s32[1,1]{1,0:T(1,128)S(6)} %copy.13.count_s, bf16[192,1536]{1,0:T(8,128)(2,1)} %bitcast.12, bf16[192,256]{1,0:T(8,128)(2,1)} %w_hbm.1, ...), custom_call_target="tpu_custom_call" | custom-call | tf_op jit(solution)/shard_map/pallas_call | solution.py:424
  67.1 0.7 copy.14
  67.8 0.7 copy.15
  68.4 0.7 copy.16
